TPU v7x, 128 devices: a whole 4x4x4 slice. The times are simulated.
128 devices in a mesh: rows: 128 (over z, x, y, core).
Axes of the slice: x: 4, y: 4, z: 4, core: 2. Of those that a mesh axis runs over, the one named last changes fastest.
Arguments:
- matrix_panel: float32 [16, 2097152], P(None, 'rows'), may hold values from -6 to 6
- row_signs: int32 [2097152], P('rows'), may hold values from -1 to 1, as said below
- sample_rows: int32 [4096], replicated, may hold values from 0 to 2097151
Outputs:
- sketch: float32 [16, 4096], P(None, 'rows')
Inputs may be any that keep to these rules, and one draw needn't show every extreme that they name: `row_signs`: each entry is -1 or 1.
All inputs are finite; a program needn't handle non-finite values.
Results may differ from a plain program's by a relative error of at most 0.00014.
Values sent between devices are 32-bit elements; how exact they have to be, the bound alone decides.
No kernel may reach another device: no remote copies, remote signals or barrier semaphores. Data moves between devices by JAX's collectives and lax.ppermute only.
A program may use at most 64 MiB of HBM per device.

v0:
```python
import math

import jax
import jax.numpy as jnp
from jax import lax
from jax.sharding import PartitionSpec as P


def partner(shard, axis, distance):
    return lax.ppermute(shard, axis, [(i, i ^ 1 << distance) for i in range(lax.axis_size(axis))])


def hadamard_table(order_size):
    indices = jnp.arange(order_size, dtype=jnp.int32)
    intersection = jnp.bitwise_and(indices[:, None], indices[None, :])
    parity = jnp.zeros((order_size, order_size), jnp.int32)
    for bit_number in range(order_size.bit_length() - 1):
        parity = parity + jnp.bitwise_and(jnp.right_shift(intersection, bit_number), 1)
    return jnp.where(parity % 2 == 0, 1.0, -1.0).astype(jnp.float32)


def local_hadamard(current):
    columns, length = current.shape
    stride = 1
    while stride < length:
        factor_size = min(128, length // stride)
        outer_count = length // (factor_size * stride)
        reshaped = current.reshape(columns, outer_count, factor_size, stride)
        reshaped = jnp.einsum(
            "cofi,gf->cogi", reshaped, hadamard_table(factor_size), precision=lax.Precision.HIGHEST
        )
        current = reshaped.reshape(columns, length)
        stride = stride * factor_size
    return current


def body(matrix_panel, row_signs, sample_rows):
    columns, length = matrix_panel.shape
    devices = lax.axis_size("rows")
    position = lax.axis_index("rows")
    levels = devices.bit_length() - 1
    signed = matrix_panel * row_signs.astype(jnp.float32)[None, :]
    local_part = local_hadamard(signed)
    upper = sample_rows // length
    lower = sample_rows % length
    bit_order = list(range(levels))
    current = local_part
    for bit_number in bit_order:
        partner_rows = partner(current, "rows", bit_number)
        my_bit = jnp.bitwise_and(jnp.right_shift(position, bit_number), 1)
        current = jnp.where(my_bit == 0, current + partner_rows, partner_rows - current)
    partials = jnp.where((upper == position)[None, :], current[:, lower], 0.0)
    collected = lax.psum_scatter(partials, "rows", scatter_dimension=1, tiled=True)
    return collected * (1.0 / math.sqrt(length * devices))


def solution(mesh):
    in_specs = (P(None, "rows"), P("rows"), P())
    out_specs = P(None, "rows")
    return jax.shard_map(body, mesh=mesh, in_specs=in_specs, out_specs=out_specs, check_vma=False)
```

profile of v0, /device:TPU:1, one launch (start us, length us, event | category | flops | bytes accessed | tf_op | source)
XLA Modules:
  0.0 954.8 jit_solution(744553146447526851)
XLA Ops:
  22.4 9.7 %subtract_select_fusion.6 = f32[16,16384]{0,1:T(8,128)} fusion(f32[16,16384]{0,1:T(8,128)} %copy.59, f32[16,16384]{0,1:T(8,128)} %copy.58, pred[]{:T(512)S(6)} %eq.46), kind=kLoop, calls=%fused_computation.7 | loop fusion | flops 786432 | bytes 3145729 | tf_op jit(solution)/shard_map/jit(_where)/select_n | solution.py:51
  32.1 5.1 copy.62
  38.7 23.4 %collective-permute-done.1 = f32[16,16384]{1,0:T(8,128)S(1)} collective-permute-done((f32[16,16384]{1,0:T(8,128)S(1)}, f32[16,16384]{1,0:T(8,128)S(1)}, u32[]{:S(2)}, u32[]{:S(2)}) %collective-permute-start.1) | collective-permute-done | bytes 1048608 | tf_op jit(solution)/shard_map/ppermute | solution.py:10
  62.1 4.6 copy.63
  66.7 9.8 %subtract_select_fusion.5 = f32[16,16384]{0,1:T(8,128)} fusion(f32[16,16384]{0,1:T(8,128)} %copy.63, f32[16,16384]{0,1:T(8,128)} %subtract_select_fusion.6, pred[]{:T(512)S(6)} %eq.45), kind=kLoop, calls=%fused_computation.6 | loop fusion | flops 786432 | bytes 3145729 | tf_op jit(solution)/shard_map/jit(_where)/select_n | solution.py:51
  76.5 5.1 copy.65
  84.7 22.5 %collective-permute-done.2 = f32[16,16384]{1,0:T(8,128)S(1)} collective-permute-done((f32[16,16384]{1,0:T(8,128)S(1)}, f32[16,16384]{1,0:T(8,128)S(1)}, u32[]{:S(2)}, u32[]{:S(2)}) %collective-permute-start.2) | collective-permute-done | bytes 1048608 | tf_op jit(solution)/shard_map/ppermute | solution.py:10
  111.7 9.7 %subtract_select_fusion.4 = f32[16,16384]{0,1:T(8,128)} fusion(f32[16,16384]{0,1:T(8,128)} %copy.66, f32[16,16384]{0,1:T(8,128)} %subtract_select_fusion.5, pred[]{:T(512)S(6)} %eq.44), kind=kLoop, calls=%fused_computation.5 | loop fusion | flops 786432 | bytes 3145729 | tf_op jit(solution)/shard_map/jit(_where)/select_n | solution.py:51
  121.5 5.1 copy.68
  127.9 21.8 %collective-permute-done.3 = f32[16,16384]{1,0:T(8,128)S(1)} collective-permute-done((f32[16,16384]{1,0:T(8,128)S(1)}, f32[16,16384]{1,0:T(8,128)S(1)}, u32[]{:S(2)}, u32[]{:S(2)}) %collective-permute-start.3) | collective-permute-done | bytes 1048608 | tf_op jit(solution)/shard_map/ppermute | solution.py:10
  149.7 4.6 copy.69
  154.3 9.8 %subtract_select_fusion.3 = f32[16,16384]{0,1:T(8,128)} fusion(f32[16,16384]{0,1:T(8,128)} %copy.69, f32[16,16384]{0,1:T(8,128)} %subtract_select_fusion.4, pred[]{:T(512)S(6)} %eq.43), kind=kLoop, calls=%fused_computation.4 | loop fusion | flops 786432 | bytes 3145729 | tf_op jit(solution)/shard_map/jit(_where)/select_n | solution.py:51
  164.1 5.1 copy.71
  172.0 20.9 %collective-permute-done.4 = f32[16,16384]{1,0:T(8,128)S(1)} collective-permute-done((f32[16,16384]{1,0:T(8,128)S(1)}, f32[16,16384]{1,0:T(8,128)S(1)}, u32[]{:S(2)}, u32[]{:S(2)}) %collective-permute-start.4) | collective-permute-done | bytes 1048608 | tf_op jit(solution)/shard_map/ppermute | solution.py:10
  197.4 9.7 %subtract_select_fusion.2 = f32[16,16384]{0,1:T(8,128)} fusion(f32[16,16384]{0,1:T(8,128)} %copy.72, f32[16,16384]{0,1:T(8,128)} %subtract_select_fusion.3, pred[]{:T(512)S(6)} %eq.42), kind=kLoop, calls=%fused_computation.3 | loop fusion | flops 786432 | bytes 3145729 | tf_op jit(solution)/shard_map/jit(_where)/select_n | solution.py:51
  207.1 5.1 copy.74
  214.1 19.8 %collective-permute-done.5 = f32[16,16384]{1,0:T(8,128)S(1)} collective-permute-done((f32[16,16384]{1,0:T(8,128)S(1)}, f32[16,16384]{1,0:T(8,128)S(1)}, u32[]{:S(2)}, u32[]{:S(2)}) %collective-permute-start.5) | collective-permute-done | bytes 1048608 | tf_op jit(solution)/shard_map/ppermute | solution.py:10
  233.9 4.6 copy.75
  238.5 9.8 %subtract_select_fusion.1 = f32[16,16384]{0,1:T(8,128)} fusion(f32[16,16384]{0,1:T(8,128)} %copy.75, f32[16,16384]{0,1:T(8,128)} %subtract_select_fusion.2, pred[]{:T(512)S(6)} %eq.41), kind=kLoop, calls=%fused_computation.2 | loop fusion | flops 786432 | bytes 3145729 | tf_op jit(solution)/shard_map/jit(_where)/select_n | solution.py:51
  248.3 5.1 copy.77
  256.8 19.0 %collective-permute-done.6 = f32[16,16384]{1,0:T(8,128)S(1)} collective-permute-done((f32[16,16384]{1,0:T(8,128)S(1)}, f32[16,16384]{1,0:T(8,128)S(1)}, u32[]{:S(2)}, u32[]{:S(2)}) %collective-permute-start.6) | collective-permute-done | bytes 1048608 | tf_op jit(solution)/shard_map/ppermute | solution.py:10
  280.4 9.7 %subtract_select_fusion = f32[16,16384]{0,1:T(8,128)} fusion(f32[16,16384]{0,1:T(8,128)} %copy.78, f32[16,16384]{0,1:T(8,128)} %subtract_select_fusion.1, pred[]{:T(512)S(6)} %eq.40), kind=kLoop, calls=%fused_computation.1 | loop fusion | flops 786432 | bytes 3145729 | tf_op jit(solution)/shard_map/jit(_where)/select_n | solution.py:51
  290.1 14.1 %gather_fusion = f32[4096,16]{1,0:T(8,128)S(1)} fusion(f32[16,16384]{0,1:T(8,128)} %subtract_select_fusion, s32[4096]{0:T(1024)S(1)} %fusion.14), kind=kCustom, calls=%fused_computation | custom fusion | bytes 540672 | tf_op jit(solution)/shard_map/gather | solution.py:52
  307.4 639.2 %reduce-scatter.4.cloned.1.call-done = f32[32,16]{1,0:T(8,128)} async-done(((f32[4096,16]{1,0:T(8,128)}), f32[32,16]{1,0:T(8,128)}) %reduce-scatter.4.cloned.1.call-update) | async-done | bytes 2064
  (28 shorter events, 48.0 us)
Async XLA Ops:
  6.5 940.1 %reduce-scatter.4.cloned.1.call-start = ((), (), s32[]{:S(2)}) async-start(), calls=%async_computation.1 | async-start | bytes 2113536
  11.7 6.1 collective-permute-start
  37.2 24.9 %collective-permute-start.1 = (f32[16,16384]{1,0:T(8,128)S(1)}, f32[16,16384]{1,0:T(8,128)S(1)}, u32[]{:S(2)}, u32[]{:S(2)}) collective-permute-start(f32[16,16384]{1,0:T(8,128)S(1)} %copy.62), channel_id=1, source_target_pairs={{0,2},{1,3},{2,0},{3,1},{4,6},{5,7},{6,4},{7,5},{8,10},{9,11},{10,... | collective-permute-start | bytes 3145736 | tf_op jit(solution)/shard_map/ppermute | solution.py:10
  81.6 25.5 %collective-permute-start.2 = (f32[16,16384]{1,0:T(8,128)S(1)}, f32[16,16384]{1,0:T(8,128)S(1)}, u32[]{:S(2)}, u32[]{:S(2)}) collective-permute-start(f32[16,16384]{1,0:T(8,128)S(1)} %copy.65), channel_id=1, source_target_pairs={{0,4},{1,5},{2,6},{3,7},{4,0},{5,1},{6,2},{7,3},{8,12},{9,13},{10,... | collective-permute-start | bytes 3145736 | tf_op jit(solution)/shard_map/ppermute | solution.py:10
  126.6 23.1 %collective-permute-start.3 = (f32[16,16384]{1,0:T(8,128)S(1)}, f32[16,16384]{1,0:T(8,128)S(1)}, u32[]{:S(2)}, u32[]{:S(2)}) collective-permute-start(f32[16,16384]{1,0:T(8,128)S(1)} %copy.68), channel_id=1, source_target_pairs={{0,8},{1,9},{2,10},{3,11},{4,12},{5,13},{6,14},{7,15},{8,0},{9,1},... | collective-permute-start | bytes 3145736 | tf_op jit(solution)/shard_map/ppermute | solution.py:10
  169.2 23.7 %collective-permute-start.4 = (f32[16,16384]{1,0:T(8,128)S(1)}, f32[16,16384]{1,0:T(8,128)S(1)}, u32[]{:S(2)}, u32[]{:S(2)}) collective-permute-start(f32[16,16384]{1,0:T(8,128)S(1)} %copy.71), channel_id=1, source_target_pairs={{0,16},{1,17},{2,18},{3,19},{4,20},{5,21},{6,22},{7,23},{8,24},{9,... | collective-permute-start | bytes 3145736 | tf_op jit(solution)/shard_map/ppermute | solution.py:10
  212.3 21.7 %collective-permute-start.5 = (f32[16,16384]{1,0:T(8,128)S(1)}, f32[16,16384]{1,0:T(8,128)S(1)}, u32[]{:S(2)}, u32[]{:S(2)}) collective-permute-start(f32[16,16384]{1,0:T(8,128)S(1)} %copy.74), channel_id=1, source_target_pairs={{0,32},{1,33},{2,34},{3,35},{4,36},{5,37},{6,38},{7,39},{8,40},{9,... | collective-permute-start | bytes 3145736 | tf_op jit(solution)/shard_map/ppermute | solution.py:10
  248.3 8.5 copy-start
  253.4 22.4 %collective-permute-start.6 = (f32[16,16384]{1,0:T(8,128)S(1)}, f32[16,16384]{1,0:T(8,128)S(1)}, u32[]{:S(2)}, u32[]{:S(2)}) collective-permute-start(f32[16,16384]{1,0:T(8,128)S(1)} %copy.77), channel_id=1, source_target_pairs={{0,64},{1,65},{2,66},{3,67},{4,68},{5,69},{6,70},{7,71},{8,72},{9,... | collective-permute-start | bytes 3145736 | tf_op jit(solution)/shard_map/ppermute | solution.py:10
Sparse Core Ops, SparseCore 0:
  307.5 639.0 reduce-scatter.3
where the time goes:
time: 962 us; the launch traced here: 955 us
  waiting for transfers between devices  766 us (80%)
  local copies, waits for them, and re-layouts  83.2 us (9%)
  other arithmetic  74.2 us (8%)
  starting transfers between devices  15.3 us (2%)
  between operations  13.5 us (1%)
    unnamed x2, waiting for transfers between devices  639 us
    ppermute x7, waiting for transfers between devices, partner(): lax.ppermute(shard, axis, [(i, i ^ 1 << distance) for i in range(lax.axis...  127 us
    select_n x7, other arithmetic, body(): jnp.where(my_bit == 0, current + partner_rows, partner_rows - current)  68.3 us
    ppermute x7, local copies, waits for them, and re-layouts, partner(): lax.ppermute(shard, axis, [(i, i ^ 1 << distance) for i in range(lax.axis...  32.2 us
    select_n x6, local copies, waits for them, and re-layouts, body(): jnp.where(my_bit == 0, current + partner_rows, partner_rows - current)  30.6 us
  transfers between devices with their start and end apart: 8, of which 7 were waited for; matrix products, arithmetic and copies ran while one was open for 0% of the time, Pallas kernels for 0%

commit v1 on v0

v1 whole, which is shorter than its diff:
```python
import functools
import math

import jax
import jax.numpy as jnp
from jax import lax
from jax.experimental import pallas as pl
from jax.experimental.pallas import tpu as pltpu
from jax.sharding import PartitionSpec as P

LANES = 128
FOLD = 256


def butterflies(parts):
    parts = list(parts)
    half = 1
    while half < len(parts):
        for i in range(len(parts)):
            if not i & half:
                low, high = parts[i], parts[i + half]
                parts[i], parts[i + half] = low + high, low - high
        half *= 2
    return parts


def odd_bits(x, width):
    shift = 1
    while shift < width:
        shift *= 2
    while shift > 1:
        shift //= 2
        x = x ^ (x >> shift)
    return x & 1


def plus_minus(bit):
    return (1 - 2 * bit).astype(jnp.float32)


def sampled_table(rows, position, local_bits):
    lower = rows & ((1 << local_bits) - 1)
    mine = plus_minus(odd_bits((rows >> local_bits) & position, 7))
    within = lower & (LANES - 1)
    sublane = lax.broadcasted_iota(jnp.int32, (8, LANES), 0)
    table = [plus_minus(odd_bits(sublane & within, 3)) * mine]
    for bit in range(3, 7):
        flip = plus_minus((within >> bit) & 1)
        table = table + [t * flip for t in table]
    return jnp.concatenate(table, axis=0).astype(jnp.bfloat16), lower >> 7


def regroup(block):
    row = lax.broadcasted_iota(jnp.int32, block.shape, 0) >> 2
    lane = lax.broadcasted_iota(jnp.int32, block.shape, 1) >> 5
    shift = (lane - row) & 3
    out = block
    for s in range(1, 4):
        turned = pltpu.roll(block, 32 * s, 1)
        turned = jnp.concatenate([turned[4 * s:], turned[:4 * s]], axis=0)
        out = jnp.where(shift == s, turned, out)
    return out


def sample_kernel(local_bits, position_ref, panel_ref, sign_ref, sample_ref, out_ref, half_ref, pair_ref):
    columns = panel_ref.shape[0]
    tiles = panel_ref.shape[1] // LANES
    inner = 8
    outer = tiles // inner
    for a in range(outer):
        parts = []
        for b in range(inner):
            tile = a * inner + b
            sign = sign_ref[tile:tile + 1, :].astype(jnp.float32)
            parts.append(panel_ref[:, tile * LANES:(tile + 1) * LANES] * sign)
        for b, part in enumerate(butterflies(parts)):
            half_ref[a * inner + b] = part
    for b in range(inner):
        parts = butterflies([half_ref[a * inner + b] for a in range(outer)])
        for a, part in enumerate(parts):
            tile = a * inner + b
            high = part.astype(jnp.bfloat16)
            low = (part - high.astype(jnp.float32)).astype(jnp.bfloat16)
            pair_ref[tile * columns:(tile + 1) * columns, :LANES] = high
            pair_ref[tile * columns:(tile + 1) * columns, LANES:] = low

    position = position_ref[0]
    groups = FOLD // LANES
    step = 256

    def one_fold(t, carry):
        tables, homes = [], []
        for g in range(groups):
            rows = sample_ref[pl.ds(t * groups + g, 1), :]
            table, home = sampled_table(rows, position, local_bits)
            tables.append(table)
            homes.append(home)
        table = jnp.concatenate(tables, axis=1)
        home = jnp.concatenate(homes, axis=1)
        table = jnp.concatenate([table, table], axis=0)
        picked = jnp.zeros((columns, FOLD), jnp.float32)
        for start in range(0, tiles * columns, step):
            values = jnp.dot(pair_ref[start:start + step, :], table, preferred_element_type=jnp.float32)
            for i in range(step // columns):
                tile = start // columns + i
                picked = jnp.where(home == tile, values[i * columns:(i + 1) * columns], picked)
        for g in range(groups):
            start = pl.multiple_of((t * groups + g) * 16, 16)
            out_ref[pl.ds(start, 16), :] = regroup(picked[:, g * LANES:(g + 1) * LANES])
        return carry

    lax.fori_loop(0, sample_ref.shape[0] // groups, one_fold, 0)


def sum_kernel(scale, parts_ref, out_ref):
    total = parts_ref[0:8, :]
    for start in range(8, parts_ref.shape[0], 8):
        total = total + parts_ref[start:start + 8, :]
    total = (total[0:4] + total[4:8]) * scale
    for j in range(4):
        out_ref[4 * j:4 * j + 4, :] = total[:, 32 * j:32 * j + 32]


def body(matrix_panel, row_signs, sample_rows):
    columns, length = matrix_panel.shape
    devices = lax.axis_size("rows")
    samples = sample_rows.shape[0]
    tiles = length // LANES
    position = lax.axis_index("rows").astype(jnp.int32).reshape(1)
    vmem = pl.BlockSpec(memory_space=pltpu.VMEM)
    partial = pl.pallas_call(
        functools.partial(sample_kernel, length.bit_length() - 1),
        out_shape=jax.ShapeDtypeStruct((samples * columns // LANES, LANES), jnp.float32),
        in_specs=[pl.BlockSpec(memory_space=pltpu.SMEM), vmem, vmem, vmem],
        out_specs=vmem,
        scratch_shapes=[
            pltpu.VMEM((tiles, columns, LANES), jnp.float32),
            pltpu.VMEM((tiles * columns, 2 * LANES), jnp.bfloat16),
        ],
        compiler_params=pltpu.CompilerParams(vmem_limit_bytes=32 * 2**20),
    )(position, matrix_panel, row_signs.reshape(tiles, LANES), sample_rows.reshape(samples // LANES, LANES))
    parts = lax.all_to_all(partial.reshape(devices, 4, LANES), "rows", 0, 0, tiled=True)
    return pl.pallas_call(
        functools.partial(sum_kernel, 1.0 / math.sqrt(length * devices)),
        out_shape=jax.ShapeDtypeStruct((columns, samples // devices), jnp.float32),
        in_specs=[vmem],
        out_specs=vmem,
    )(parts.reshape(devices * 4, LANES))


def solution(mesh):
    in_specs = (P(None, "rows"), P("rows"), P())
    out_specs = P(None, "rows")
    return jax.shard_map(body, mesh=mesh, in_specs=in_specs, out_specs=out_specs, check_vma=False)
```

time: 962 us -> 37.1 us (0.04)
  waiting for transfers between devices: 766 us -> 0 us
  local copies, waits for them, and re-layouts: 83.2 us -> 2.78 us
  other arithmetic: 74.2 us -> 0 us
  blocking collectives: 0 us -> 22.5 us
  starting transfers between devices: 15.3 us -> 0 us
  between operations: 13.5 us -> 0.01 us
  Pallas kernels: 0 us -> 11.6 us
    unnamed x2 -> x0, waiting for transfers between devices: 639 us -> none
    ppermute x7 -> x0, waiting for transfers between devices: 127 us -> none  [partner(): lax.ppermute(shard, axis, [(i, i ^ 1 << distance) for i in range(lax.axis...]
    select_n x8 -> x0, other arithmetic: 71.4 us -> none  [the longest x7 68.3 us: body(): jnp.where(my_bit == 0, current + partner_rows, partner_rows - current)]
    ppermute x7 -> x0, local copies, waits for them, and re-layouts: 32.2 us -> none  [partner(): lax.ppermute(shard, axis, [(i, i ^ 1 << distance) for i in range(lax.axis...]
    select_n x6 -> x0, local copies, waits for them, and re-layouts: 30.6 us -> none  [body(): jnp.where(my_bit == 0, current + partner_rows, partner_rows - current)]
    all_to_all x0 -> x1, blocking collectives: none -> 22.5 us  [body(): lax.all_to_all(partial.reshape(devices, 4, LANES), 'rows', 0, 0, tiled=True)]
    ppermute x7 -> x0, starting transfers between devices: 15.3 us -> none  [partner(): lax.ppermute(shard, axis, [(i, i ^ 1 << distance) for i in range(lax.axis...]
    gather x1 -> x0, local copies, waits for them, and re-layouts: 14.1 us -> none  [body(): partials = jnp.where((upper == position)[None, :], current[:, lower], 0.0)]
  transfers between devices with their start and end apart: 8 -> 0, of which waited for: 7 -> 0; matrix products, arithmetic and copies ran while one was open for 0% -> 0% of each run, Pallas kernels for 0% -> 0%
where the time goes in v1:
time: 37.1 us; the launch traced here: 36.9 us
  blocking collectives  22.5 us (61%)
  Pallas kernels  11.6 us (31%)
  local copies, waits for them, and re-layouts  2.78 us (7%)
    all_to_all x1, blocking collectives, body(): lax.all_to_all(partial.reshape(devices, 4, LANES), 'rows', 0, 0, tiled=True)  22.5 us
    pallas_call x1, Pallas kernels, body(): pl.pallas_call(functools.partial(sample_kernel, length.bit_length() - 1),...  9.89 us
    unnamed x6, local copies, waits for them, and re-layouts  2.78 us
    pallas_call x1, Pallas kernels, body(): pl.pallas_call(functools.partial(sum_kernel, 1.0 / math.sqrt(length * dev...  1.69 us

profile of v1, /device:TPU:1, one launch (start us, length us, event | category | flops | bytes accessed | tf_op | source)
XLA Modules:
  0.0 36.9 jit_solution(8524217492384304104)
XLA Ops:
  0.0 0.0 copy-start
  0.0 1.2 %copy-done = f32[16,16384]{1,0:T(8,128)S(1)} copy-done((f32[16,16384]{1,0:T(8,128)S(1)}, f32[16,16384]{1,0:T(8,128)}, u32[]{:S(2)}) %copy-start) | copy-done | bytes 1048600
  1.2 0.0 copy-start.1
  1.2 0.8 %copy-done.1 = s32[16384]{0:T(1024)S(1)} copy-done((s32[16384]{0:T(1024)S(1)}, s32[16384]{0:T(1024)}, u32[]{:S(2)}) %copy-start.1) | copy-done | bytes 65560
  2.1 0.0 copy-start.2
  2.1 0.7 %copy-done.2 = s32[4096]{0:T(1024)S(1)} copy-done((s32[4096]{0:T(1024)S(1)}, s32[4096]{0:T(1024)}, u32[]{:S(2)}) %copy-start.2) | copy-done | bytes 16408
  2.8 9.9 %shard_map.37 = f32[512,128]{1,0:T(8,128)S(1)} custom-call(s32[1]{0:T(128)} %bitcast.position_ref, f32[16,16384]{1,0:T(8,128)S(1)} %copy-done, s32[128,128]{1,0:T(8,128)S(1)} %bitcast.6, s32[32,128]{1,0:T(8,128)S(1)} %bitcast.7), custom_call_target="tpu_custom_call" | custom-call | tf_op jit(solution)/shard_map/pallas_call | solution.py:131
  12.7 22.5 %all_to_all.5 = f32[128,4,128]{2,1,0:T(4,128)} all-to-all(f32[128,4,128]{2,1,0:T(4,128)S(1)} %bitcast.5), channel_id=1, replica_groups=mesh['rows'=128] {'rows'}, dimensions={0} | all-to-all | bytes 524288 | tf_op jit(solution)/shard_map/all_to_all | solution.py:142
  35.2 1.7 %shard_map.38 = f32[16,32]{1,0:T(8,128)} custom-call(f32[512,128]{1,0:T(8,128)} %bitcast.8), custom_call_target="tpu_custom_call" | custom-call | tf_op jit(solution)/shard_map/pallas_call | solution.py:143
Async XLA Ops:
  0.0 1.2 %copy-start = (f32[16,16384]{1,0:T(8,128)S(1)}, f32[16,16384]{1,0:T(8,128)}, u32[]{:S(2)}) copy-start(f32[16,16384]{1,0:T(8,128)} %panel_ref.1) | copy-start | bytes 3145732
  1.2 0.8 %copy-start.1 = (s32[16384]{0:T(1024)S(1)}, s32[16384]{0:T(1024)}, u32[]{:S(2)}) copy-start(s32[16384]{0:T(1024)} %param.4) | copy-start | bytes 196612
  2.1 0.7 %copy-start.2 = (s32[4096]{0:T(1024)S(1)}, s32[4096]{0:T(1024)}, u32[]{:S(2)}) copy-start(s32[4096]{0:T(1024)} %param.5) | copy-start | bytes 49156

commit v2 on v1

--- a/solution.py
+++ b/solution.py
@@ -62,12 +62,34 @@
     return out
 
 
-def sample_kernel(local_bits, position_ref, panel_ref, sign_ref, sample_ref, out_ref, half_ref, pair_ref):
-    columns = panel_ref.shape[0]
-    tiles = panel_ref.shape[1] // LANES
+def sample_kernel(local_bits, position_ref, panel_hbm, sign_hbm, sample_hbm, out_hbm, panel_ref, sign_ref, sample_ref, half_ref, pair_ref, table_ref, home_ref, out_ref, panel_sems, out_sems, sems):
+    columns, length = panel_ref.shape
+    tiles = length // LANES
     inner = 8
     outer = tiles // inner
+    sample_copy = pltpu.make_async_copy(sample_hbm, sample_ref, sems.at[0])
+    sample_copy.start()
+    sign_copy = pltpu.make_async_copy(sign_hbm, sign_ref, sems.at[1])
+    sign_copy.start()
+    pieces = panel_sems.shape[0]
+    width = length // pieces
+    panel_copies = []
+    for p in range(pieces):
+        part = pl.ds(p * width, width)
+        panel_copies.append(pltpu.make_async_copy(panel_hbm.at[:, part], panel_ref.at[:, part], panel_sems.at[p]))
+        panel_copies[-1].start()
+
+    position = position_ref[0]
+    sample_copy.wait()
+    for g in range(sample_ref.shape[0]):
+        table, home = sampled_table(sample_ref[g:g + 1, :], position, local_bits)
+        table_ref[:, g * LANES:(g + 1) * LANES] = table
+        home_ref[g:g + 1, :] = home
+
+    sign_copy.wait()
     for a in range(outer):
+        if a % (outer // pieces) == 0:
+            panel_copies[a // (outer // pieces)].wait()
         parts = []
         for b in range(inner):
             tile = a * inner + b
@@ -84,20 +106,16 @@
             pair_ref[tile * columns:(tile + 1) * columns, :LANES] = high
             pair_ref[tile * columns:(tile + 1) * columns, LANES:] = low
 
-    position = position_ref[0]
     groups = FOLD // LANES
     step = 256
-
-    def one_fold(t, carry):
-        tables, homes = [], []
-        for g in range(groups):
-            rows = sample_ref[pl.ds(t * groups + g, 1), :]
-            table, home = sampled_table(rows, position, local_bits)
-            tables.append(table)
-            homes.append(home)
-        table = jnp.concatenate(tables, axis=1)
-        home = jnp.concatenate(homes, axis=1)
+    folds = sample_ref.shape[0] // groups
+    out_pieces = out_sems.shape[0]
+    out_rows = out_ref.shape[0] // out_pieces
+    out_copies = []
+    for t in range(folds):
+        table = table_ref[:, t * FOLD:(t + 1) * FOLD]
         table = jnp.concatenate([table, table], axis=0)
+        home = jnp.concatenate([home_ref[t * groups + g:t * groups + g + 1, :] for g in range(groups)], axis=1)
         picked = jnp.zeros((columns, FOLD), jnp.float32)
         for start in range(0, tiles * columns, step):
             values = jnp.dot(pair_ref[start:start + step, :], table, preferred_element_type=jnp.float32)
@@ -105,20 +123,15 @@
                 tile = start // columns + i
                 picked = jnp.where(home == tile, values[i * columns:(i + 1) * columns], picked)
         for g in range(groups):
-            start = pl.multiple_of((t * groups + g) * 16, 16)
-            out_ref[pl.ds(start, 16), :] = regroup(picked[:, g * LANES:(g + 1) * LANES])
-        return carry
-
-    lax.fori_loop(0, sample_ref.shape[0] // groups, one_fold, 0)
-
-
-def sum_kernel(scale, parts_ref, out_ref):
-    total = parts_ref[0:8, :]
-    for start in range(8, parts_ref.shape[0], 8):
-        total = total + parts_ref[start:start + 8, :]
-    total = (total[0:4] + total[4:8]) * scale
-    for j in range(4):
-        out_ref[4 * j:4 * j + 4, :] = total[:, 32 * j:32 * j + 32]
+            row = (t * groups + g) * 16
+            out_ref[row:row + 16, :] = regroup(picked[:, g * LANES:(g + 1) * LANES])
+        if (t + 1) % (folds // out_pieces) == 0:
+            p = len(out_copies)
+            part = pl.ds(p * out_rows, out_rows)
+            out_copies.append(pltpu.make_async_copy(out_ref.at[part], out_hbm.at[part], out_sems.at[p]))
+            out_copies[-1].start()
+    for copy in out_copies:
+        copy.wait()
 
 
 def body(matrix_panel, row_signs, sample_rows):
@@ -127,25 +140,31 @@
     samples = sample_rows.shape[0]
     tiles = length // LANES
     position = lax.axis_index("rows").astype(jnp.int32).reshape(1)
-    vmem = pl.BlockSpec(memory_space=pltpu.VMEM)
+    hbm = pl.BlockSpec(memory_space=pltpu.HBM)
+    groups = samples // LANES
     partial = pl.pallas_call(
         functools.partial(sample_kernel, length.bit_length() - 1),
         out_shape=jax.ShapeDtypeStruct((samples * columns // LANES, LANES), jnp.float32),
-        in_specs=[pl.BlockSpec(memory_space=pltpu.SMEM), vmem, vmem, vmem],
-        out_specs=vmem,
+        in_specs=[pl.BlockSpec(memory_space=pltpu.SMEM), hbm, hbm, hbm],
+        out_specs=hbm,
         scratch_shapes=[
+            pltpu.VMEM((columns, length), jnp.float32),
+            pltpu.VMEM((tiles, LANES), jnp.int32),
+            pltpu.VMEM((groups, LANES), jnp.int32),
             pltpu.VMEM((tiles, columns, LANES), jnp.float32),
             pltpu.VMEM((tiles * columns, 2 * LANES), jnp.bfloat16),
+            pltpu.VMEM((LANES, samples), jnp.bfloat16),
+            pltpu.VMEM((groups, LANES), jnp.int32),
+            pltpu.VMEM((samples * columns // LANES, LANES), jnp.float32),
+            pltpu.SemaphoreType.DMA((4,)),
+            pltpu.SemaphoreType.DMA((8,)),
+            pltpu.SemaphoreType.DMA((2,)),
         ],
-        compiler_params=pltpu.CompilerParams(vmem_limit_bytes=32 * 2**20),
-    )(position, matrix_panel, row_signs.reshape(tiles, LANES), sample_rows.reshape(samples // LANES, LANES))
+        compiler_params=pltpu.CompilerParams(vmem_limit_bytes=62 * 2**20),
+    )(position, matrix_panel, row_signs.reshape(tiles, LANES), sample_rows.reshape(groups, LANES))
     parts = lax.all_to_all(partial.reshape(devices, 4, LANES), "rows", 0, 0, tiled=True)
-    return pl.pallas_call(
-        functools.partial(sum_kernel, 1.0 / math.sqrt(length * devices)),
-        out_shape=jax.ShapeDtypeStruct((columns, samples // devices), jnp.float32),
-        in_specs=[vmem],
-        out_specs=vmem,
-    )(parts.reshape(devices * 4, LANES))
+    total = jnp.sum(parts, axis=0) * (1.0 / math.sqrt(length * devices))
+    return jnp.concatenate([total[:, 32 * j:32 * j + 32] for j in range(4)], axis=0)
 
 
 def solution(mesh):

time: 37.1 us -> 32 us (0.86)
  Pallas kernels: 11.6 us -> 8.36 us
  local copies, waits for them, and re-layouts: 2.78 us -> 0.08 us
  other arithmetic: 0 us -> 0.76 us
    unnamed x6 -> x0, local copies, waits for them, and re-layouts: 2.78 us -> none
    pallas_call x1 -> x0, Pallas kernels: 1.69 us -> none  [body(): pl.pallas_call(functools.partial(sum_kernel, 1.0 / math.sqrt(length * dev...]
    pallas_call x1, Pallas kernels: 9.89 us -> 8.36 us  [body(): pl.pallas_call(functools.partial(sample_kernel, length.bit_length() - 1),...]
    concatenate x0 -> x1, other arithmetic: none -> 0.61 us  [body(): jnp.concatenate([total[:, 32 * j:32 * j + 32] for j in range(4)], axis=0)]
where the time goes in v2:
time: 32 us; the launch traced here: 31.8 us
  blocking collectives  22.6 us (71%)
  Pallas kernels  8.36 us (26%)
  other arithmetic  0.76 us (2%)
    all_to_all x1, blocking collectives, body(): lax.all_to_all(partial.reshape(devices, 4, LANES), 'rows', 0, 0, tiled=True)  22.6 us
    pallas_call x1, Pallas kernels, body(): pl.pallas_call(functools.partial(sample_kernel, length.bit_length() - 1),...  8.36 us

profile of v2, /device:TPU:1, one launch (start us, length us, event | category | flops | bytes accessed | tf_op | source)
XLA Modules:
  0.0 31.8 jit_solution(4103996973338323303)
XLA Ops:
  0.0 8.4 %shard_map.37 = f32[512,128]{1,0:T(8,128)} custom-call(s32[1]{0:T(128)} %bitcast.position_ref, f32[16,16384]{1,0:T(8,128)} %panel_hbm.1, s32[128,128]{1,0:T(8,128)} %bitcast.5, s32[32,128]{1,0:T(8,128)} %bitcast.6), custom_call_target="tpu_custom_call" | custom-call | tf_op jit(solution)/shard_map/pallas_call | solution.py:145
  8.4 22.6 %all_to_all.5 = f32[128,4,128]{2,1,0:T(4,128)S(1)} all-to-all(f32[128,4,128]{2,1,0:T(4,128)} %bitcast.4), channel_id=1, replica_groups=mesh['rows'=128] {'rows'}, dimensions={0} | all-to-all | bytes 524288 | tf_op jit(solution)/shard_map/all_to_all | solution.py:165
  31.0 0.1 reduce_sum.9
  31.1 0.1 fusion
  31.2 0.6 %pad_maximum_fusion = f32[16,32]{1,0:T(8,128)} fusion(f32[4,32]{1,0:T(4,128)S(1)} %get-tuple-element.6, f32[4,32]{1,0:T(4,128)S(1)} %get-tuple-element.7, f32[4,32]{1,0:T(4,128)S(1)} %get-tuple-element.8, f32[4,32]{1,0:T(4,128)S(1)} %get-tuple-element.5), kind=kLoop, calls=%fused_computation | loop fusion | flops 1536 | bytes 4096 | tf_op jit(solution)/shard_map/concatenate | solution.py:167
  (1 shorter events, 0.0 us)

commit v3 on v1

v3 whole, which is shorter than its diff:
```python
import functools
import math

import jax
import jax.numpy as jnp
from jax import lax
from jax.experimental import pallas as pl
from jax.experimental.pallas import tpu as pltpu
from jax.sharding import PartitionSpec as P

LANES = 128
FOLD = 256


def butterflies(parts):
    parts = list(parts)
    half = 1
    while half < len(parts):
        for i in range(len(parts)):
            if not i & half:
                low, high = parts[i], parts[i + half]
                parts[i], parts[i + half] = low + high, low - high
        half *= 2
    return parts


def odd_bits(x, width):
    shift = 1
    while shift < width:
        shift *= 2
    while shift > 1:
        shift //= 2
        x = x ^ (x >> shift)
    return x & 1


def plus_minus(bit):
    return (1 - 2 * bit).astype(jnp.float32)


def sampled_table(rows, position, local_bits):
    lower = rows & ((1 << local_bits) - 1)
    mine = plus_minus(odd_bits((rows >> local_bits) & position, 7))
    within = lower & (LANES - 1)
    sublane = lax.broadcasted_iota(jnp.int32, (8, LANES), 0)
    table = [plus_minus(odd_bits(sublane & within, 3)) * mine]
    for bit in range(3, 7):
        flip = plus_minus((within >> bit) & 1)
        table = table + [t * flip for t in table]
    return jnp.concatenate(table, axis=0).astype(jnp.bfloat16), lower >> 7


def regroup(block):
    row = lax.broadcasted_iota(jnp.int32, block.shape, 0) >> 2
    lane = lax.broadcasted_iota(jnp.int32, block.shape, 1) >> 5
    shift = (lane - row) & 3
    out = block
    for s in range(1, 4):
        turned = pltpu.roll(block, 32 * s, 1)
        turned = jnp.concatenate([turned[4 * s:], turned[:4 * s]], axis=0)
        out = jnp.where(shift == s, turned, out)
    return out


def choose(blocks, masks):
    for mask in masks:
        blocks = [jnp.where(mask, high, low) for low, high in zip(blocks[::2], blocks[1::2])]
    return blocks[0]


def sample_kernel(local_bits, position_ref, panel_ref, sign_ref, sample_ref, out_ref, half_ref, pair_ref):
    columns, length = panel_ref.shape
    tiles = length // LANES
    inner = 8
    outer = tiles // inner
    position = position_ref[0]
    for a in range(outer):
        parts = []
        for b in range(inner):
            tile = a * inner + b
            sign = sign_ref[tile:tile + 1, :].astype(jnp.float32)
            parts.append(panel_ref[:, tile * LANES:(tile + 1) * LANES] * sign)
        for b, part in enumerate(butterflies(parts)):
            half_ref[b * outer + a] = part
    for b in range(inner):
        parts = butterflies([half_ref[b * outer + a] for a in range(outer)])
        for a, part in enumerate(parts):
            row = (b * outer + a) * columns
            high = part.astype(jnp.bfloat16)
            low = (part - high.astype(jnp.float32)).astype(jnp.bfloat16)
            pair_ref[row:row + columns, :LANES] = high
            pair_ref[row:row + columns, LANES:] = low

    groups = FOLD // LANES
    step = outer * columns
    for t in range(sample_ref.shape[0] // groups):
        tables, masks = [], []
        for g in range(groups):
            row = t * groups + g
            table, home = sampled_table(sample_ref[row:row + 1, :], position, local_bits)
            tables.append(table)
            home = jnp.broadcast_to(home, (8, LANES))
            masks.append([(home & (1 << bit)) != 0 for bit in range(7)])
        table = jnp.concatenate(tables, axis=1)
        table = jnp.concatenate([table, table], axis=0)
        picked = {}
        for b in range(inner):
            values = jnp.dot(pair_ref[b * step:(b + 1) * step, :], table, preferred_element_type=jnp.float32)
            for g in range(groups):
                for h in range(0, columns, 8):
                    lanes = slice(g * LANES, (g + 1) * LANES)
                    blocks = [values[a * columns + h:a * columns + h + 8, lanes] for a in range(outer)]
                    picked[b, g, h] = choose(blocks, masks[g][3:])
        for g in range(groups):
            row = (t * groups + g) * columns
            chosen = [choose([picked[b, g, h] for b in range(inner)], masks[g][:3]) for h in range(0, columns, 8)]
            out_ref[row:row + columns, :] = regroup(jnp.concatenate(chosen, axis=0))


def body(matrix_panel, row_signs, sample_rows):
    columns, length = matrix_panel.shape
    devices = lax.axis_size("rows")
    samples = sample_rows.shape[0]
    tiles = length // LANES
    position = lax.axis_index("rows").astype(jnp.int32).reshape(1)
    vmem = pl.BlockSpec(memory_space=pltpu.VMEM)
    groups = samples // LANES
    partial = pl.pallas_call(
        functools.partial(sample_kernel, length.bit_length() - 1),
        out_shape=jax.ShapeDtypeStruct((samples * columns // LANES, LANES), jnp.float32),
        in_specs=[pl.BlockSpec(memory_space=pltpu.SMEM), vmem, vmem, vmem],
        out_specs=vmem,
        scratch_shapes=[
            pltpu.VMEM((tiles, columns, LANES), jnp.float32),
            pltpu.VMEM((tiles * columns, 2 * LANES), jnp.bfloat16),
        ],
        compiler_params=pltpu.CompilerParams(vmem_limit_bytes=32 * 2**20),
    )(position, -matrix_panel, row_signs.reshape(tiles, LANES), sample_rows.reshape(groups, LANES))
    parts = lax.all_to_all(partial.reshape(devices, 4, LANES), "rows", 0, 0, tiled=True)
    total = jnp.sum(parts, axis=0) * (-1.0 / math.sqrt(length * devices))
    return jnp.concatenate([total[:, 32 * j:32 * j + 32] for j in range(4)], axis=0)


def solution(mesh):
    in_specs = (P(None, "rows"), P("rows"), P())
    out_specs = P(None, "rows")
    return jax.shard_map(body, mesh=mesh, in_specs=in_specs, out_specs=out_specs, check_vma=False)
```

time: 37.1 us -> 29.8 us (0.80)
  Pallas kernels: 11.6 us -> 5.07 us
  local copies, waits for them, and re-layouts: 2.78 us -> 0.08 us
  other arithmetic: 0 us -> 2.09 us
    pallas_call x1, Pallas kernels: 9.89 us -> 5.07 us  [body(): pl.pallas_call(functools.partial(sample_kernel, length.bit_length() - 1),...]
    unnamed x6 -> x4, local copies, waits for them, and re-layouts: 2.78 us -> 0.01 us
    pallas_call x1 -> x0, Pallas kernels: 1.69 us -> none  [body(): pl.pallas_call(functools.partial(sum_kernel, 1.0 / math.sqrt(length * dev...]
    neg x0 -> x1, other arithmetic: none -> 1.33 us  [body(): -matrix_panel]
    concatenate x0 -> x1, other arithmetic: none -> 0.61 us  [body(): jnp.concatenate([total[:, 32 * j:32 * j + 32] for j in range(4)], axis=0)]
where the time goes in v3:
time: 29.8 us; the launch traced here: 29.7 us
  blocking collectives  22.4 us (75%)
  Pallas kernels  5.07 us (17%)
  other arithmetic  2.09 us (7%)
    all_to_all x1, blocking collectives, body(): lax.all_to_all(partial.reshape(devices, 4, LANES), 'rows', 0, 0, tiled=True)  22.4 us
    pallas_call x1, Pallas kernels, body(): pl.pallas_call(functools.partial(sample_kernel, length.bit_length() - 1),...  5.07 us
    neg x1, other arithmetic, body(): -matrix_panel  1.33 us
    concatenate x1, other arithmetic, body(): jnp.concatenate([total[:, 32 * j:32 * j + 32] for j in range(4)], axis=0)  0.61 us

profile of v3, /device:TPU:1, one launch (start us, length us, event | category | flops | bytes accessed | tf_op | source)
XLA Modules:
  0.0 29.7 jit_solution(3397886105862534555)
XLA Ops:
  0.0 0.0 copy-start
  0.0 0.0 copy-start.1
  0.0 1.3 %neg.3.panel_ref = f32[16,16384]{1,0:T(8,128)S(1)} negate(f32[16,16384]{1,0:T(8,128)} %param.3) | non-fusion elementwise | flops 262144 | bytes 2097152 | tf_op jit(solution)/shard_map/neg | solution.py:138
  1.3 0.0 copy-done
  1.3 0.0 copy-done.1
  1.4 5.1 %shard_map.37 = f32[512,128]{1,0:T(8,128)S(1)} custom-call(s32[1]{0:T(128)} %bitcast.position_ref, f32[16,16384]{1,0:T(8,128)S(1)} %neg.3.panel_ref, s32[128,128]{1,0:T(8,128)S(1)} %bitcast.5, s32[32,128]{1,0:T(8,128)S(1)} %bitcast.6), custom_call_target="tpu_custom_call" | custom-call | tf_op jit(solution)/shard_map/pallas_call | solution.py:128
  6.4 22.4 %all_to_all.5 = f32[128,4,128]{2,1,0:T(4,128)S(1)} all-to-all(f32[128,4,128]{2,1,0:T(4,128)S(1)} %bitcast.4), channel_id=1, replica_groups=mesh['rows'=128] {'rows'}, dimensions={0} | all-to-all | bytes 524288 | tf_op jit(solution)/shard_map/all_to_all | solution.py:139
  28.8 0.1 reduce_sum.9
  29.0 0.1 fusion
  29.1 0.6 %pad_maximum_fusion = f32[16,32]{1,0:T(8,128)} fusion(f32[4,32]{1,0:T(4,128)S(1)} %get-tuple-element.6, f32[4,32]{1,0:T(4,128)S(1)} %get-tuple-element.7, f32[4,32]{1,0:T(4,128)S(1)} %get-tuple-element.8, f32[4,32]{1,0:T(4,128)S(1)} %get-tuple-element.5), kind=kLoop, calls=%fused_computation | loop fusion | flops 1536 | bytes 4096 | tf_op jit(solution)/shard_map/concatenate | solution.py:141
  (1 shorter events, 0.0 us)
Async XLA Ops:
  0.0 1.3 %copy-start = (s32[16384]{0:T(1024)S(1)}, s32[16384]{0:T(1024)}, u32[]{:S(2)}) copy-start(s32[16384]{0:T(1024)} %param.4) | copy-start | bytes 196612
  0.0 1.3 %copy-start.1 = (s32[4096]{0:T(1024)S(1)}, s32[4096]{0:T(1024)}, u32[]{:S(2)}) copy-start(s32[4096]{0:T(1024)} %param.5) | copy-start | bytes 49156

commit v4 on v3

--- a/solution.py
+++ b/solution.py
@@ -10,6 +10,8 @@
 
 LANES = 128
 FOLD = 256
+CHIP_ORDER = (2, 0, 3, 1)
+FIRST_CHIP = 42
 
 
 def butterflies(parts):
@@ -68,7 +70,46 @@
     return blocks[0]
 
 
-def sample_kernel(local_bits, position_ref, panel_ref, sign_ref, sample_ref, out_ref, half_ref, pair_ref):
+def samples_of_core(sample_ref, core):
+    samples = sample_ref[...]
+    samples = jnp.where(core == 0, samples, pltpu.roll(samples, 96, 1))
+    turned = pltpu.roll(samples, 32, 1)
+    block = lax.broadcasted_iota(jnp.int32, (1, LANES), 1) >> 5
+    return [
+        jnp.where((block & 1) == 0, samples[2 * g + 1:2 * g + 2], turned[2 * g:2 * g + 1])
+        for g in range(samples.shape[0] // 2)
+    ]
+
+
+def sample_folds(rows, position, local_bits, columns, pair_ref, out_ref):
+    inner = 8
+    outer = (1 << local_bits) // LANES // inner
+    groups = FOLD // LANES
+    step = outer * columns
+    for t in range(len(rows) // groups):
+        tables, masks = [], []
+        for g in range(groups):
+            table, home = sampled_table(rows[t * groups + g], position, local_bits)
+            tables.append(table)
+            home = jnp.broadcast_to(home, (8, LANES))
+            masks.append([(home & (1 << bit)) != 0 for bit in range(7)])
+        table = jnp.concatenate(tables, axis=1)
+        table = jnp.concatenate([table, table], axis=0)
+        picked = {}
+        for b in range(inner):
+            values = jnp.dot(pair_ref[b * step:(b + 1) * step, :], table, preferred_element_type=jnp.float32)
+            for g in range(groups):
+                for h in range(0, columns, 8):
+                    lanes = slice(g * LANES, (g + 1) * LANES)
+                    blocks = [values[a * columns + h:a * columns + h + 8, lanes] for a in range(outer)]
+                    picked[b, g, h] = choose(blocks, masks[g][3:])
+        for g in range(groups):
+            row = ((t * groups + g) ^ (FIRST_CHIP // 4)) * columns
+            chosen = [choose([picked[b, g, h] for b in range(inner)], masks[g][:3]) for h in range(0, columns, 8)]
+            out_ref[row:row + columns, :] = regroup(jnp.concatenate(chosen, axis=0))
+
+
+def partner_kernel(local_bits, position_ref, panel_ref, sign_ref, sample_ref, out_ref, pair_ref, half_ref):
     columns, length = panel_ref.shape
     tiles = length // LANES
     inner = 8
@@ -90,53 +131,51 @@
             low = (part - high.astype(jnp.float32)).astype(jnp.bfloat16)
             pair_ref[row:row + columns, :LANES] = high
             pair_ref[row:row + columns, LANES:] = low
+    rows = samples_of_core(sample_ref, 1 - (position & 1))
+    sample_folds(rows, position, local_bits, columns, pair_ref, out_ref)
 
-    groups = FOLD // LANES
-    step = outer * columns
-    for t in range(sample_ref.shape[0] // groups):
-        tables, masks = [], []
-        for g in range(groups):
-            row = t * groups + g
-            table, home = sampled_table(sample_ref[row:row + 1, :], position, local_bits)
-            tables.append(table)
-            home = jnp.broadcast_to(home, (8, LANES))
-            masks.append([(home & (1 << bit)) != 0 for bit in range(7)])
-        table = jnp.concatenate(tables, axis=1)
-        table = jnp.concatenate([table, table], axis=0)
-        picked = {}
-        for b in range(inner):
-            values = jnp.dot(pair_ref[b * step:(b + 1) * step, :], table, preferred_element_type=jnp.float32)
-            for g in range(groups):
-                for h in range(0, columns, 8):
-                    lanes = slice(g * LANES, (g + 1) * LANES)
-                    blocks = [values[a * columns + h:a * columns + h + 8, lanes] for a in range(outer)]
-                    picked[b, g, h] = choose(blocks, masks[g][3:])
-        for g in range(groups):
-            row = (t * groups + g) * columns
-            chosen = [choose([picked[b, g, h] for b in range(inner)], masks[g][:3]) for h in range(0, columns, 8)]
-            out_ref[row:row + columns, :] = regroup(jnp.concatenate(chosen, axis=0))
+
+def own_kernel(local_bits, columns, position_ref, pair_ref, sample_ref, out_ref):
+    position = position_ref[0]
+    rows = samples_of_core(sample_ref, position & 1)
+    sample_folds(rows, position, local_bits, columns, pair_ref, out_ref)
 
 
 def body(matrix_panel, row_signs, sample_rows):
     columns, length = matrix_panel.shape
     devices = lax.axis_size("rows")
+    chips = devices // 2
     samples = sample_rows.shape[0]
     tiles = length // LANES
+    local_bits = length.bit_length() - 1
     position = lax.axis_index("rows").astype(jnp.int32).reshape(1)
+    sample_rows = sample_rows.reshape(samples // LANES, LANES)
+    smem = pl.BlockSpec(memory_space=pltpu.SMEM)
     vmem = pl.BlockSpec(memory_space=pltpu.VMEM)
-    groups = samples // LANES
-    partial = pl.pallas_call(
-        functools.partial(sample_kernel, length.bit_length() - 1),
-        out_shape=jax.ShapeDtypeStruct((samples * columns // LANES, LANES), jnp.float32),
-        in_specs=[pl.BlockSpec(memory_space=pltpu.SMEM), vmem, vmem, vmem],
+    params = pltpu.CompilerParams(vmem_limit_bytes=32 * 2**20)
+    half_shape = jax.ShapeDtypeStruct((samples * columns // LANES // 2, LANES), jnp.float32)
+    work = samples * columns * length
+    partner, pair = pl.pallas_call(
+        functools.partial(partner_kernel, local_bits),
+        out_shape=(half_shape, jax.ShapeDtypeStruct((tiles * columns, 2 * LANES), jnp.bfloat16)),
+        in_specs=[smem, vmem, vmem, vmem],
+        out_specs=(vmem, vmem),
+        scratch_shapes=[pltpu.VMEM((tiles, columns, LANES), jnp.float32)],
+        compiler_params=params,
+        cost_estimate=pl.CostEstimate(flops=2 * work, bytes_accessed=2**21, transcendentals=0),
+    )(position, -matrix_panel, row_signs.reshape(tiles, LANES), sample_rows)
+    arrived = lax.ppermute(partner.reshape(chips, 4, LANES), "rows", [(i, i ^ 1) for i in range(devices)])
+    own = pl.pallas_call(
+        functools.partial(own_kernel, local_bits, columns),
+        out_shape=half_shape,
+        in_specs=[smem, vmem, vmem],
         out_specs=vmem,
-        scratch_shapes=[
-            pltpu.VMEM((tiles, columns, LANES), jnp.float32),
-            pltpu.VMEM((tiles * columns, 2 * LANES), jnp.bfloat16),
-        ],
-        compiler_params=pltpu.CompilerParams(vmem_limit_bytes=32 * 2**20),
-    )(position, -matrix_panel, row_signs.reshape(tiles, LANES), sample_rows.reshape(groups, LANES))
-    parts = lax.all_to_all(partial.reshape(devices, 4, LANES), "rows", 0, 0, tiled=True)
+        compiler_params=params,
+        cost_estimate=pl.CostEstimate(flops=2 * work, bytes_accessed=2**21, transcendentals=0),
+    )(position, pair, sample_rows)
+    partial = own.reshape(chips, 4, LANES) + arrived
+    order = [4 * (p ^ (FIRST_CHIP // 4)) + chip for p in range(chips // 4) for chip in CHIP_ORDER]
+    parts = lax.all_to_all(partial, "rows", 0, 0, axis_index_groups=[[2 * chip + core for chip in order] for core in range(2)], tiled=True)
     total = jnp.sum(parts, axis=0) * (-1.0 / math.sqrt(length * devices))
     return jnp.concatenate([total[:, 32 * j:32 * j + 32] for j in range(4)], axis=0)
 

time: 29.8 us -> 24.8 us (0.83)
  blocking collectives: 22.4 us -> 15.3 us
  starting transfers between devices: 0 us -> 1.5 us
  Pallas kernels: 5.07 us -> 5.69 us
    all_to_all x1, blocking collectives: 22.4 us -> 15.3 us  [body(): lax.all_to_all(partial, 'rows', 0, 0, axis_index_groups=[[2 * chip + core...]
    ppermute x0 -> x1, starting transfers between devices: none -> 1.5 us  [body(): lax.ppermute(partner.reshape(chips, 4, LANES), 'rows', [(i, i ^ 1) for i...]
    pallas_call x1 -> x2, Pallas kernels: 5.07 us -> 5.69 us  [the longest x1 3.05 us: body(): pl.pallas_call(functools.partial(partner_kernel, local_bits), out_shape=(...]
  transfers between devices with their start and end apart: 0 -> 1, of which waited for: 0 -> 0; matrix products, arithmetic and copies ran while one was open for 0% -> 0% of each run, Pallas kernels for 0% -> 11%
where the time goes in v4:
time: 24.8 us; the launch traced here: 24.6 us
  blocking collectives  15.3 us (62%)
  Pallas kernels  5.69 us (23%)
  other arithmetic  2.06 us (8%)
  starting transfers between devices  1.5 us (6%)
    all_to_all x1, blocking collectives, body(): lax.all_to_all(partial, 'rows', 0, 0, axis_index_groups=[[2 * chip + core...  15.3 us
    pallas_call x1, Pallas kernels, body(): pl.pallas_call(functools.partial(partner_kernel, local_bits), out_shape=(...  3.05 us
    pallas_call x1, Pallas kernels, body(): pl.pallas_call(functools.partial(own_kernel, local_bits, columns), out_sh...  2.64 us
    ppermute x1, starting transfers between devices, body(): lax.ppermute(partner.reshape(chips, 4, LANES), 'rows', [(i, i ^ 1) for i...  1.5 us
    neg x1, other arithmetic, body(): -matrix_panel  1.33 us
    concatenate x1, other arithmetic, body(): jnp.concatenate([total[:, 32 * j:32 * j + 32] for j in range(4)], axis=0)  0.61 us
  transfers between devices with their start and end apart: 1, of which 0 were waited for; matrix products, arithmetic and copies ran while one was open for 0% of the time, Pallas kernels for 11%

profile of v4, /device:TPU:1, one launch (start us, length us, event | category | flops | bytes accessed | tf_op | source)
XLA Modules:
  0.0 24.6 jit_solution(4003615887882682756)
XLA Ops:
  0.0 0.0 copy-start
  0.0 0.0 copy-start.1
  0.0 1.3 %neg.3.panel_ref = f32[16,16384]{1,0:T(8,128)S(1)} negate(f32[16,16384]{1,0:T(8,128)} %param.3) | non-fusion elementwise | flops 262144 | bytes 2097152 | tf_op jit(solution)/shard_map/neg | solution.py:166
  1.3 0.0 copy-done
  1.3 0.0 copy-done.1
  1.4 3.0 %shard_map.37 = (f32[256,128]{1,0:T(8,128)S(1)}, bf16[2048,256]{1,0:T(8,128)(2,1)S(1)}) custom-call(s32[1]{0:T(128)} %bitcast.position_ref, f32[16,16384]{1,0:T(8,128)S(1)} %neg.3.panel_ref, s32[128,128]{1,0:T(8,128)S(1)} %bitcast.7, s32[32,128]{1,0:T(8,128)S(1)} %bitcast.8), custom_call_target="tpu_custom_call" | custom-call | flops 2147483648 | bytes 2097152 | tf_op jit(solution)/shard_map/pallas_call | solution.py:158
  4.4 1.5 %collective-permute-start = (f32[64,4,128]{2,1,0:T(4,128)S(1)}, f32[64,4,128]{2,1,0:T(4,128)S(1)}, u32[]{:S(2)}, u32[]{:S(2)}) collective-permute-start(f32[64,4,128]{2,1,0:T(4,128)S(1)} %bitcast.6), channel_id=1, source_target_pairs={{0,1},{1,0},{2,3},{3,2},{4,5},{5,4},{6,7},{7,6},{8,9},{9,8},{10,11... | collective-permute-start | bytes 393224 | tf_op jit(solution)/shard_map/ppermute | solution.py:167
  5.9 2.6 %shard_map.38 = f32[256,128]{1,0:T(8,128)S(1)} custom-call(s32[1]{0:T(128)} %bitcast.position_ref, bf16[2048,256]{1,0:T(8,128)(2,1)S(1)} %get-tuple-element.7.pair_ref, s32[32,128]{1,0:T(8,128)S(1)} %bitcast.9), custom_call_target="tpu_custom_call" | custom-call | flops 2147483648 | bytes 2097152 | tf_op jit(solution)/shard_map/pallas_call | solution.py:168
  8.6 0.0 collective-permute-done
  8.6 15.3 %all_to_all.5 = f32[64,4,128]{2,1,0:T(4,128)S(1)} all-to-all(f32[64,4,128]{2,1,0:T(4,128)S(1)} %add.3), channel_id=1, replica_groups={{84,80,86,82,92,88,94,90,68,64,70,66,76,72,78,74,116,112,118,114,124,12..., dimensions={0} | all-to-all | bytes 262144 | tf_op jit(solution)/shard_map/all_to_all | solution.py:178
  23.9 0.1 reduce_sum.9
  24.0 0.1 fusion
  24.0 0.6 %pad_maximum_fusion = f32[16,32]{1,0:T(8,128)} fusion(f32[4,32]{1,0:T(4,128)S(1)} %get-tuple-element.10, f32[4,32]{1,0:T(4,128)S(1)} %get-tuple-element.11, f32[4,32]{1,0:T(4,128)S(1)} %get-tuple-element.12, f32[4,32]{1,0:T(4,128)S(1)} %get-tuple-element.9), kind=kLoop, calls=%fused_computation | loop fusion | flops 1536 | bytes 4096 | tf_op jit(solution)/shard_map/concatenate | solution.py:180
  (2 shorter events, 0.0 us)
Async XLA Ops:
  0.0 1.3 %copy-start = (s32[16384]{0:T(1024)S(1)}, s32[16384]{0:T(1024)}, u32[]{:S(2)}) copy-start(s32[16384]{0:T(1024)} %param.4) | copy-start | bytes 196612
  0.0 1.3 %copy-start.1 = (s32[4096]{0:T(1024)S(1)}, s32[4096]{0:T(1024)}, u32[]{:S(2)}) copy-start(s32[4096]{0:T(1024)} %param.5) | copy-start | bytes 49156
  4.4 4.2 %collective-permute-start = (f32[64,4,128]{2,1,0:T(4,128)S(1)}, f32[64,4,128]{2,1,0:T(4,128)S(1)}, u32[]{:S(2)}, u32[]{:S(2)}) collective-permute-start(f32[64,4,128]{2,1,0:T(4,128)S(1)} %bitcast.6), channel_id=1, source_target_pairs={{0,1},{1,0},{2,3},{3,2},{4,5},{5,4},{6,7},{7,6},{8,9},{9,8},{10,11... | collective-permute-start | bytes 393224 | tf_op jit(solution)/shard_map/ppermute | solution.py:167

commit v5 on v4

--- a/solution.py
+++ b/solution.py
@@ -12,6 +12,8 @@
 FOLD = 256
 CHIP_ORDER = (2, 0, 3, 1)
 FIRST_CHIP = 42
+PARTNER_LOOKUPS = 14
+OWN_LOOKUPS = 10
 
 
 def butterflies(parts):
@@ -41,15 +43,13 @@
 
 
 def sampled_table(rows, position, local_bits):
-    lower = rows & ((1 << local_bits) - 1)
-    mine = plus_minus(odd_bits((rows >> local_bits) & position, 7))
-    within = lower & (LANES - 1)
+    within = rows & (LANES - 1)
     sublane = lax.broadcasted_iota(jnp.int32, (8, LANES), 0)
-    table = [plus_minus(odd_bits(sublane & within, 3)) * mine]
+    table = [plus_minus(odd_bits(sublane & within, 3)) * sample_sign(rows, position, local_bits)]
     for bit in range(3, 7):
         flip = plus_minus((within >> bit) & 1)
         table = table + [t * flip for t in table]
-    return jnp.concatenate(table, axis=0).astype(jnp.bfloat16), lower >> 7
+    return jnp.concatenate(table, axis=0).astype(jnp.bfloat16)
 
 
 def regroup(block):
@@ -81,40 +81,100 @@
     ]
 
 
-def sample_folds(rows, position, local_bits, columns, pair_ref, out_ref):
+def sample_sign(rows, position, local_bits):
+    return plus_minus(odd_bits((rows >> local_bits) & position, 7))
+
+
+def tile_masks(rows, local_bits):
+    tile = jnp.broadcast_to((rows & ((1 << local_bits) - 1)) >> 7, (8, LANES))
+    return [(tile & (1 << bit)) != 0 for bit in range(7)]
+
+
+def store_group(group, chosen, out_ref):
+    chosen = jnp.concatenate(chosen, axis=0)
+    row = (group ^ (FIRST_CHIP // 4)) * chosen.shape[0]
+    out_ref[row:row + chosen.shape[0], :] = regroup(chosen)
+
+
+def matmul_fold(rows, first, position, local_bits, columns, pair_ref, out_ref):
     inner = 8
     outer = (1 << local_bits) // LANES // inner
-    groups = FOLD // LANES
     step = outer * columns
-    for t in range(len(rows) // groups):
-        tables, masks = [], []
-        for g in range(groups):
-            table, home = sampled_table(rows[t * groups + g], position, local_bits)
-            tables.append(table)
-            home = jnp.broadcast_to(home, (8, LANES))
-            masks.append([(home & (1 << bit)) != 0 for bit in range(7)])
-        table = jnp.concatenate(tables, axis=1)
-        table = jnp.concatenate([table, table], axis=0)
-        picked = {}
-        for b in range(inner):
-            values = jnp.dot(pair_ref[b * step:(b + 1) * step, :], table, preferred_element_type=jnp.float32)
-            for g in range(groups):
-                for h in range(0, columns, 8):
-                    lanes = slice(g * LANES, (g + 1) * LANES)
-                    blocks = [values[a * columns + h:a * columns + h + 8, lanes] for a in range(outer)]
-                    picked[b, g, h] = choose(blocks, masks[g][3:])
-        for g in range(groups):
-            row = ((t * groups + g) ^ (FIRST_CHIP // 4)) * columns
-            chosen = [choose([picked[b, g, h] for b in range(inner)], masks[g][:3]) for h in range(0, columns, 8)]
-            out_ref[row:row + columns, :] = regroup(jnp.concatenate(chosen, axis=0))
-
-
-def partner_kernel(local_bits, position_ref, panel_ref, sign_ref, sample_ref, out_ref, pair_ref, half_ref):
+    table = jnp.concatenate([sampled_table(row, position, local_bits) for row in rows], axis=1)
+    table = jnp.concatenate([table, table], axis=0)
+    masks = [tile_masks(row, local_bits) for row in rows]
+    picked = {}
+    for b in range(inner):
+        values = jnp.dot(pair_ref[b * step:(b + 1) * step, :], table, preferred_element_type=jnp.float32)
+        for g in range(len(rows)):
+            for h in range(0, columns, 8):
+                lanes = slice(g * LANES, (g + 1) * LANES)
+                blocks = [values[a * columns + h:a * columns + h + 8, lanes] for a in range(outer)]
+                picked[b, g, h] = choose(blocks, masks[g][3:])
+    for g in range(len(rows)):
+        chosen = [choose([picked[b, g, h] for b in range(inner)], masks[g][:3]) for h in range(0, columns, 8)]
+        store_group(first + g, chosen, out_ref)
+
+
+def whole_table(columns, pair_ref, whole_ref):
+    place = lax.broadcasted_iota(jnp.int32, (LANES, LANES), 0)
+    lane = lax.broadcasted_iota(jnp.int32, (LANES, LANES), 1)
+    signs = plus_minus(odd_bits(place & lane, 7)).astype(jnp.bfloat16)
+    signs = jnp.concatenate([signs, signs], axis=1)
+    step = 2 * LANES
+    for b in range(pair_ref.shape[0] // step):
+        part = lax.dot_general(
+            signs, pair_ref[b * step:(b + 1) * step, :], (((1,), (1,)), ((), ())), preferred_element_type=jnp.float32
+        )
+        whole_ref[8 + b * step:8 + b * step + LANES, :] = part[:, :LANES]
+        whole_ref[8 + b * step + LANES:8 + (b + 1) * step, :] = part[:, LANES:]
+
+
+def whole_rows(rows, local_bits):
+    lower = rows & ((1 << local_bits) - 1)
+    tile = lower >> 7
+    sublane = lax.broadcasted_iota(jnp.int32, rows.shape, 1) & 7
+    return (((((tile & 7) << 1) | (tile >> 6)) << 7) | (lower & (LANES - 1))) + 8 - sublane
+
+
+def lookup_group(row, group, slot, position, local_bits, columns, index_ref, whole_ref, out_ref):
+    base = slot * LANES
+    sublane = lax.broadcasted_iota(jnp.int32, (8, LANES), 0)
+    blocks = []
+    for k in range(0, LANES, 8):
+        lines = whole_ref[pl.ds(index_ref[slot, k], 8), :]
+        for j in range(1, 8):
+            lines = jnp.where(sublane == j, whole_ref[pl.ds(index_ref[slot, k + j], 8), :], lines)
+        blocks.append(lines)
+    values = jnp.concatenate(blocks, axis=0).T
+    masks = tile_masks(row, local_bits)[3:6]
+    mine = jnp.broadcast_to(sample_sign(row, position, local_bits), (8, LANES))
+    chosen = [
+        choose([values[a * columns + h:a * columns + h + 8] for a in range(8)], masks) * mine
+        for h in range(0, columns, 8)
+    ]
+    store_group(group, chosen, out_ref)
+
+
+def matmul_all(rows, lookups, position, local_bits, columns, pair_ref, out_ref):
+    for g in range(lookups, len(rows), 2):
+        matmul_fold(rows[g:g + 2], g, position, local_bits, columns, pair_ref, out_ref)
+
+
+def partner_kernel(local_bits, position_ref, panel_ref, sign_ref, sample_ref, out_ref, own_ref, pair_ref, half_ref, whole_ref, place_ref, index_ref, sem):
     columns, length = panel_ref.shape
     tiles = length // LANES
     inner = 8
     outer = tiles // inner
     position = position_ref[0]
+    rows = samples_of_core(sample_ref, 1 - (position & 1))
+    own_rows = samples_of_core(sample_ref, position & 1)
+    lookups = [(row, g, out_ref) for g, row in enumerate(rows[:PARTNER_LOOKUPS])]
+    lookups += [(row, g, own_ref) for g, row in enumerate(own_rows[:OWN_LOOKUPS])]
+    for slot, (row, _, _) in enumerate(lookups):
+        place_ref[slot:slot + 1, :] = whole_rows(row, local_bits)
+    copy = pltpu.make_async_copy(place_ref, index_ref, sem)
+    copy.start()
     for a in range(outer):
         parts = []
         for b in range(inner):
@@ -131,14 +191,20 @@
             low = (part - high.astype(jnp.float32)).astype(jnp.bfloat16)
             pair_ref[row:row + columns, :LANES] = high
             pair_ref[row:row + columns, LANES:] = low
-    rows = samples_of_core(sample_ref, 1 - (position & 1))
-    sample_folds(rows, position, local_bits, columns, pair_ref, out_ref)
-
-
-def own_kernel(local_bits, columns, position_ref, pair_ref, sample_ref, out_ref):
+    whole_table(columns, pair_ref, whole_ref)
+    matmul_all(rows, PARTNER_LOOKUPS, position, local_bits, columns, pair_ref, out_ref)
+    copy.wait()
+    for slot, (row, group, target) in enumerate(lookups):
+        lookup_group(row, group, slot, position, local_bits, columns, index_ref, whole_ref, target)
+
+
+def own_kernel(local_bits, columns, position_ref, pair_ref, own_ref, sample_ref, out_ref):
     position = position_ref[0]
     rows = samples_of_core(sample_ref, position & 1)
-    sample_folds(rows, position, local_bits, columns, pair_ref, out_ref)
+    for g in range(OWN_LOOKUPS):
+        start = (g ^ (FIRST_CHIP // 4)) * columns
+        out_ref[start:start + columns, :] = own_ref[start:start + columns, :]
+    matmul_all(rows, OWN_LOOKUPS, position, local_bits, columns, pair_ref, out_ref)
 
 
 def body(matrix_panel, row_signs, sample_rows):
@@ -155,12 +221,19 @@
     params = pltpu.CompilerParams(vmem_limit_bytes=32 * 2**20)
     half_shape = jax.ShapeDtypeStruct((samples * columns // LANES // 2, LANES), jnp.float32)
     work = samples * columns * length
-    partner, pair = pl.pallas_call(
+    lookups = PARTNER_LOOKUPS + OWN_LOOKUPS
+    partner, own, pair = pl.pallas_call(
         functools.partial(partner_kernel, local_bits),
-        out_shape=(half_shape, jax.ShapeDtypeStruct((tiles * columns, 2 * LANES), jnp.bfloat16)),
+        out_shape=(half_shape, half_shape, jax.ShapeDtypeStruct((tiles * columns, 2 * LANES), jnp.bfloat16)),
         in_specs=[smem, vmem, vmem, vmem],
-        out_specs=(vmem, vmem),
-        scratch_shapes=[pltpu.VMEM((tiles, columns, LANES), jnp.float32)],
+        out_specs=(vmem, vmem, vmem),
+        scratch_shapes=[
+            pltpu.VMEM((tiles, columns, LANES), jnp.float32),
+            pltpu.VMEM((tiles * columns + 16, LANES), jnp.float32),
+            pltpu.VMEM((lookups, LANES), jnp.int32),
+            pltpu.SMEM((lookups, LANES), jnp.int32),
+            pltpu.SemaphoreType.DMA,
+        ],
         compiler_params=params,
         cost_estimate=pl.CostEstimate(flops=2 * work, bytes_accessed=2**21, transcendentals=0),
     )(position, -matrix_panel, row_signs.reshape(tiles, LANES), sample_rows)
@@ -168,11 +241,11 @@
     own = pl.pallas_call(
         functools.partial(own_kernel, local_bits, columns),
         out_shape=half_shape,
-        in_specs=[smem, vmem, vmem],
+        in_specs=[smem, vmem, vmem, vmem],
         out_specs=vmem,
         compiler_params=params,
         cost_estimate=pl.CostEstimate(flops=2 * work, bytes_accessed=2**21, transcendentals=0),
-    )(position, pair, sample_rows)
+    )(position, pair, own, sample_rows)
     partial = own.reshape(chips, 4, LANES) + arrived
     order = [4 * (p ^ (FIRST_CHIP // 4)) + chip for p in range(chips // 4) for chip in CHIP_ORDER]
     parts = lax.all_to_all(partial, "rows", 0, 0, axis_index_groups=[[2 * chip + core for chip in order] for core in range(2)], tiled=True)

time: 24.8 us -> 24 us (0.968)
  Pallas kernels: 5.69 us -> 4.91 us
    pallas_call x1, Pallas kernels: 2.64 us -> 1.25 us  [body(): pl.pallas_call(functools.partial(own_kernel, local_bits, columns), out_sh...]
    pallas_call x1, Pallas kernels: 3.05 us -> 3.66 us  [body(): pl.pallas_call(functools.partial(partner_kernel, local_bits), out_shape=(...]
  transfers between devices with their start and end apart: 1 -> 1, of which waited for: 0 -> 0; matrix products, arithmetic and copies ran while one was open for 0% -> 0% of each run, Pallas kernels for 11% -> 5%
where the time goes in v5:
time: 24 us; the launch traced here: 23.9 us
  blocking collectives  15.3 us (64%)
  Pallas kernels  4.91 us (20%)
  other arithmetic  2.06 us (9%)
  starting transfers between devices  1.5 us (6%)
    all_to_all x1, blocking collectives, body(): lax.all_to_all(partial, 'rows', 0, 0, axis_index_groups=[[2 * chip + core...  15.3 us
    pallas_call x1, Pallas kernels, body(): pl.pallas_call(functools.partial(partner_kernel, local_bits), out_shape=(...  3.66 us
    ppermute x1, starting transfers between devices, body(): lax.ppermute(partner.reshape(chips, 4, LANES), 'rows', [(i, i ^ 1) for i...  1.5 us
    neg x1, other arithmetic, body(): -matrix_panel  1.33 us
    pallas_call x1, Pallas kernels, body(): pl.pallas_call(functools.partial(own_kernel, local_bits, columns), out_sh...  1.25 us
    concatenate x1, other arithmetic, body(): jnp.concatenate([total[:, 32 * j:32 * j + 32] for j in range(4)], axis=0)  0.61 us
  transfers between devices with their start and end apart: 1, of which 0 were waited for; matrix products, arithmetic and copies ran while one was open for 0% of the time, Pallas kernels for 5%

profile of v5, /device:TPU:1, one launch (start us, length us, event | category | flops | bytes accessed | tf_op | source)
XLA Modules:
  0.0 23.9 jit_solution(2151515020606822165)
XLA Ops:
  0.0 0.0 copy-start
  0.0 0.0 copy-start.1
  0.0 1.3 %neg.3.panel_ref = f32[16,16384]{1,0:T(8,128)S(1)} negate(f32[16,16384]{1,0:T(8,128)} %param.3) | non-fusion elementwise | flops 262144 | bytes 2097152 | tf_op jit(solution)/shard_map/neg | solution.py:239
  1.3 0.0 copy-done
  1.3 0.0 copy-done.1
  1.4 3.7 %shard_map.37 = (f32[256,128]{1,0:T(8,128)S(1)}, f32[256,128]{1,0:T(8,128)S(1)}, bf16[2048,256]{1,0:T(8,128)(2,1)S(1)}) custom-call(s32[1]{0:T(128)} %bitcast.position_ref, f32[16,16384]{1,0:T(8,128)S(1)} %neg.3.panel_ref, s32[128,128]{1,0:T(8,128)S(1)} %bitcast.7, s32[32,128]{1,0:T(8,128)S(1)} %bitcast.8), custom_call_target="tpu_custom_call" | custom-call | flops 2147483648 | bytes 2097152 | tf_op jit(solution)/shard_map/pallas_call | solution.py:225
  5.0 1.5 %collective-permute-start = (f32[64,4,128]{2,1,0:T(4,128)S(1)}, f32[64,4,128]{2,1,0:T(4,128)S(1)}, u32[]{:S(2)}, u32[]{:S(2)}) collective-permute-start(f32[64,4,128]{2,1,0:T(4,128)S(1)} %bitcast.6), channel_id=1, source_target_pairs={{0,1},{1,0},{2,3},{3,2},{4,5},{5,4},{6,7},{7,6},{8,9},{9,8},{10,11... | collective-permute-start | bytes 393224 | tf_op jit(solution)/shard_map/ppermute | solution.py:240
  6.5 1.3 %shard_map.38 = f32[256,128]{1,0:T(8,128)S(1)} custom-call(s32[1]{0:T(128)} %bitcast.position_ref, bf16[2048,256]{1,0:T(8,128)(2,1)S(1)} %get-tuple-element.8.pair_ref, f32[256,128]{1,0:T(8,128)S(1)} %get-tuple-element.9.own_ref, s32[32,128]{1,0:T(8,128)S(1)} %bitcast.9), custom_call_target="tpu_custom_call" | custom-call | flops 2147483648 | bytes 2097152 | tf_op jit(solution)/shard_map/pallas_call | solution.py:241
  7.8 0.0 collective-permute-done
  7.8 15.3 %all_to_all.5 = f32[64,4,128]{2,1,0:T(4,128)S(1)} all-to-all(f32[64,4,128]{2,1,0:T(4,128)S(1)} %add.3), channel_id=1, replica_groups={{84,80,86,82,92,88,94,90,68,64,70,66,76,72,78,74,116,112,118,114,124,12..., dimensions={0} | all-to-all | bytes 262144 | tf_op jit(solution)/shard_map/all_to_all | solution.py:251
  23.1 0.1 reduce_sum.9
  23.2 0.1 fusion
  23.3 0.6 %pad_maximum_fusion = f32[16,32]{1,0:T(8,128)} fusion(f32[4,32]{1,0:T(4,128)S(1)} %get-tuple-element.12, f32[4,32]{1,0:T(4,128)S(1)} %get-tuple-element.13, f32[4,32]{1,0:T(4,128)S(1)} %get-tuple-element.14, f32[4,32]{1,0:T(4,128)S(1)} %get-tuple-element.11), kind=kLoop, calls=%fused_computation | loop fusion | flops 1536 | bytes 4096 | tf_op jit(solution)/shard_map/concatenate | solution.py:253
  (2 shorter events, 0.0 us)
Async XLA Ops:
  0.0 1.3 %copy-start = (s32[16384]{0:T(1024)S(1)}, s32[16384]{0:T(1024)}, u32[]{:S(2)}) copy-start(s32[16384]{0:T(1024)} %param.4) | copy-start | bytes 196612
  0.0 1.3 %copy-start.1 = (s32[4096]{0:T(1024)S(1)}, s32[4096]{0:T(1024)}, u32[]{:S(2)}) copy-start(s32[4096]{0:T(1024)} %param.5) | copy-start | bytes 49156
  5.0 2.8 %collective-permute-start = (f32[64,4,128]{2,1,0:T(4,128)S(1)}, f32[64,4,128]{2,1,0:T(4,128)S(1)}, u32[]{:S(2)}, u32[]{:S(2)}) collective-permute-start(f32[64,4,128]{2,1,0:T(4,128)S(1)} %bitcast.6), channel_id=1, source_target_pairs={{0,1},{1,0},{2,3},{3,2},{4,5},{5,4},{6,7},{7,6},{8,9},{9,8},{10,11... | collective-permute-start | bytes 393224 | tf_op jit(solution)/shard_map/ppermute | solution.py:240

commit v6 on v5

--- a/solution.py
+++ b/solution.py
@@ -12,7 +12,8 @@
 FOLD = 256
 CHIP_ORDER = (2, 0, 3, 1)
 FIRST_CHIP = 42
-PARTNER_LOOKUPS = 14
+UNROLL = 4
+PARTNER_LOOKUPS = 16
 OWN_LOOKUPS = 10
 
 
@@ -175,14 +176,18 @@
         place_ref[slot:slot + 1, :] = whole_rows(row, local_bits)
     copy = pltpu.make_async_copy(place_ref, index_ref, sem)
     copy.start()
-    for a in range(outer):
+
+    def first_half(a, carry):
         parts = []
         for b in range(inner):
             tile = a * inner + b
-            sign = sign_ref[tile:tile + 1, :].astype(jnp.float32)
-            parts.append(panel_ref[:, tile * LANES:(tile + 1) * LANES] * sign)
+            sign = sign_ref[pl.ds(tile, 1), :].astype(jnp.float32)
+            parts.append(panel_ref[:, pl.ds(pl.multiple_of(tile * LANES, LANES), LANES)] * sign)
         for b, part in enumerate(butterflies(parts)):
             half_ref[b * outer + a] = part
+        return carry
+
+    lax.fori_loop(0, outer, first_half, 0, unroll=UNROLL)
     for b in range(inner):
         parts = butterflies([half_ref[b * outer + a] for a in range(outer)])
         for a, part in enumerate(parts):
@@ -205,6 +210,15 @@
         start = (g ^ (FIRST_CHIP // 4)) * columns
         out_ref[start:start + columns, :] = own_ref[start:start + columns, :]
     matmul_all(rows, OWN_LOOKUPS, position, local_bits, columns, pair_ref, out_ref)
+
+
+def sum_kernel(scale, parts_ref, out_ref):
+    total = parts_ref[0:8, :]
+    for start in range(8, parts_ref.shape[0], 8):
+        total = total + parts_ref[start:start + 8, :]
+    total = (total[0:4] + total[4:8]) * scale
+    for j in range(4):
+        out_ref[4 * j:4 * j + 4, :] = total[:, 32 * j:32 * j + 32]
 
 
 def body(matrix_panel, row_signs, sample_rows):
@@ -249,8 +263,13 @@
     partial = own.reshape(chips, 4, LANES) + arrived
     order = [4 * (p ^ (FIRST_CHIP // 4)) + chip for p in range(chips // 4) for chip in CHIP_ORDER]
     parts = lax.all_to_all(partial, "rows", 0, 0, axis_index_groups=[[2 * chip + core for chip in order] for core in range(2)], tiled=True)
-    total = jnp.sum(parts, axis=0) * (-1.0 / math.sqrt(length * devices))
-    return jnp.concatenate([total[:, 32 * j:32 * j + 32] for j in range(4)], axis=0)
+    return pl.pallas_call(
+        functools.partial(sum_kernel, -1.0 / math.sqrt(length * devices)),
+        out_shape=jax.ShapeDtypeStruct((columns, samples // devices), jnp.float32),
+        in_specs=[vmem],
+        out_specs=vmem,
+        compiler_params=params,
+    )(parts.reshape(chips * 4, LANES))
 
 
 def solution(mesh):

time: 24 us -> 23.3 us (0.971)
  other arithmetic: 2.06 us -> 1.36 us
    pallas_call x0 -> x1, Pallas kernels: none -> 0.7 us  [body(): pl.pallas_call(functools.partial(sum_kernel, -1.0 / math.sqrt(length * de...]
    pallas_call x1, Pallas kernels: 3.66 us -> 2.97 us  [body(): pl.pallas_call(functools.partial(partner_kernel, local_bits), out_shape=(...]
    concatenate x1 -> x0, other arithmetic: 0.61 us -> none  [body(): jnp.concatenate([total[:, 32 * j:32 * j + 32] for j in range(4)], axis=0)]
where the time goes in v6:
time: 23.3 us; the launch traced here: 23.1 us
  blocking collectives  15.3 us (66%)
  Pallas kernels  4.92 us (21%)
  starting transfers between devices  1.5 us (6%)
  other arithmetic  1.36 us (6%)
    all_to_all x1, blocking collectives, body(): lax.all_to_all(partial, 'rows', 0, 0, axis_index_groups=[[2 * chip + core...  15.3 us
    pallas_call x1, Pallas kernels, body(): pl.pallas_call(functools.partial(partner_kernel, local_bits), out_shape=(...  2.97 us
    ppermute x1, starting transfers between devices, body(): lax.ppermute(partner.reshape(chips, 4, LANES), 'rows', [(i, i ^ 1) for i...  1.5 us
    neg x1, other arithmetic, body(): -matrix_panel  1.33 us
    pallas_call x1, Pallas kernels, body(): pl.pallas_call(functools.partial(own_kernel, local_bits, columns), out_sh...  1.25 us
    pallas_call x1, Pallas kernels, body(): pl.pallas_call(functools.partial(sum_kernel, -1.0 / math.sqrt(length * de...  0.7 us
  transfers between devices with their start and end apart: 1, of which 0 were waited for; matrix products, arithmetic and copies ran while one was open for 0% of the time, Pallas kernels for 5%

profile of v6, /device:TPU:1, one launch (start us, length us, event | category | flops | bytes accessed | tf_op | source)
XLA Modules:
  0.0 23.1 jit_solution(15984312965184687741)
XLA Ops:
  0.0 0.0 copy-start
  0.0 0.0 copy-start.1
  0.0 1.3 %neg.3.panel_ref = f32[16,16384]{1,0:T(8,128)S(1)} negate(f32[16,16384]{1,0:T(8,128)} %param.3) | non-fusion elementwise | flops 262144 | bytes 2097152 | tf_op jit(solution)/shard_map/neg | solution.py:253
  1.3 0.0 copy-done
  1.3 0.0 copy-done.1
  1.4 3.0 %shard_map.37 = (f32[256,128]{1,0:T(8,128)S(1)}, f32[256,128]{1,0:T(8,128)S(1)}, bf16[2048,256]{1,0:T(8,128)(2,1)S(1)}) custom-call(s32[1]{0:T(128)} %bitcast.position_ref, f32[16,16384]{1,0:T(8,128)S(1)} %neg.3.panel_ref, s32[128,128]{1,0:T(8,128)S(1)} %bitcast.9, s32[32,128]{1,0:T(8,128)S(1)} %bitcast.10), custom_call_target="tpu_custom_call" | custom-call | flops 2147483648 | bytes 2097152 | tf_op jit(solution)/shard_map/pallas_call | solution.py:239
  4.3 1.5 %collective-permute-start = (f32[64,4,128]{2,1,0:T(4,128)S(1)}, f32[64,4,128]{2,1,0:T(4,128)S(1)}, u32[]{:S(2)}, u32[]{:S(2)}) collective-permute-start(f32[64,4,128]{2,1,0:T(4,128)S(1)} %bitcast.8), channel_id=1, source_target_pairs={{0,1},{1,0},{2,3},{3,2},{4,5},{5,4},{6,7},{7,6},{8,9},{9,8},{10,11... | collective-permute-start | bytes 393224 | tf_op jit(solution)/shard_map/ppermute | solution.py:254
  5.8 1.2 %shard_map.38 = f32[256,128]{1,0:T(8,128)S(1)} custom-call(s32[1]{0:T(128)} %bitcast.position_ref, bf16[2048,256]{1,0:T(8,128)(2,1)S(1)} %get-tuple-element.8.pair_ref, f32[256,128]{1,0:T(8,128)S(1)} %get-tuple-element.9.own_ref, s32[32,128]{1,0:T(8,128)S(1)} %bitcast.11), custom_call_target="tpu_custom_call" | custom-call | flops 2147483648 | bytes 2097152 | tf_op jit(solution)/shard_map/pallas_call | solution.py:255
  7.1 0.0 collective-permute-done
  7.1 15.3 %all_to_all.5 = f32[64,4,128]{2,1,0:T(4,128)S(1)} all-to-all(f32[64,4,128]{2,1,0:T(4,128)S(1)} %add.3), channel_id=1, replica_groups={{84,80,86,82,92,88,94,90,68,64,70,66,76,72,78,74,116,112,118,114,124,12..., dimensions={0} | all-to-all | bytes 262144 | tf_op jit(solution)/shard_map/all_to_all | solution.py:265
  22.4 0.7 %shard_map.39 = f32[16,32]{1,0:T(8,128)} custom-call(f32[256,128]{1,0:T(8,128)S(1)} %bitcast.6), custom_call_target="tpu_custom_call" | custom-call | tf_op jit(solution)/shard_map/pallas_call | solution.py:266
  (1 shorter events, 0.0 us)
Async XLA Ops:
  0.0 1.3 %copy-start = (s32[16384]{0:T(1024)S(1)}, s32[16384]{0:T(1024)}, u32[]{:S(2)}) copy-start(s32[16384]{0:T(1024)} %param.4) | copy-start | bytes 196612
  0.0 1.3 %copy-start.1 = (s32[4096]{0:T(1024)S(1)}, s32[4096]{0:T(1024)}, u32[]{:S(2)}) copy-start(s32[4096]{0:T(1024)} %param.5) | copy-start | bytes 49156
  4.3 2.8 %collective-permute-start = (f32[64,4,128]{2,1,0:T(4,128)S(1)}, f32[64,4,128]{2,1,0:T(4,128)S(1)}, u32[]{:S(2)}, u32[]{:S(2)}) collective-permute-start(f32[64,4,128]{2,1,0:T(4,128)S(1)} %bitcast.8), channel_id=1, source_target_pairs={{0,1},{1,0},{2,3},{3,2},{4,5},{5,4},{6,7},{7,6},{8,9},{9,8},{10,11... | collective-permute-start | bytes 393224 | tf_op jit(solution)/shard_map/ppermute | solution.py:254

commit v7 on v6

--- a/solution.py
+++ b/solution.py
@@ -11,10 +11,11 @@
 LANES = 128
 FOLD = 256
 CHIP_ORDER = (2, 0, 3, 1)
-FIRST_CHIP = 42
+FIRST_CHIP = 58
 UNROLL = 4
 PARTNER_LOOKUPS = 16
 OWN_LOOKUPS = 10
+SHARED = 6
 
 
 def butterflies(parts):
@@ -162,7 +163,7 @@
         matmul_fold(rows[g:g + 2], g, position, local_bits, columns, pair_ref, out_ref)
 
 
-def partner_kernel(local_bits, position_ref, panel_ref, sign_ref, sample_ref, out_ref, own_ref, pair_ref, half_ref, whole_ref, place_ref, index_ref, sem):
+def partner_kernel(local_bits, position_ref, panel_ref, sign_ref, sample_ref, out_ref, own_ref, pair_ref, whole_ref, half_ref, place_ref, index_ref, sem):
     columns, length = panel_ref.shape
     tiles = length // LANES
     inner = 8
@@ -199,17 +200,43 @@
     whole_table(columns, pair_ref, whole_ref)
     matmul_all(rows, PARTNER_LOOKUPS, position, local_bits, columns, pair_ref, out_ref)
     copy.wait()
-    for slot, (row, group, target) in enumerate(lookups):
+    for slot, (row, group, target) in enumerate(lookups[:PARTNER_LOOKUPS + SHARED]):
         lookup_group(row, group, slot, position, local_bits, columns, index_ref, whole_ref, target)
 
-
-def own_kernel(local_bits, columns, position_ref, pair_ref, own_ref, sample_ref, out_ref):
+    @pl.when((position & 1) == 1)
+    def _():
+        for slot, (row, group, target) in enumerate(lookups):
+            if slot >= PARTNER_LOOKUPS + SHARED:
+                lookup_group(row, group, slot, position, local_bits, columns, index_ref, whole_ref, target)
+
+
+def own_kernel(local_bits, columns, position_ref, pair_ref, whole_ref, own_ref, sample_ref, out_ref, place_ref, index_ref, sem):
     position = position_ref[0]
     rows = samples_of_core(sample_ref, position & 1)
-    for g in range(OWN_LOOKUPS):
-        start = (g ^ (FIRST_CHIP // 4)) * columns
-        out_ref[start:start + columns, :] = own_ref[start:start + columns, :]
-    matmul_all(rows, OWN_LOOKUPS, position, local_bits, columns, pair_ref, out_ref)
+    for g in range(SHARED, OWN_LOOKUPS):
+        place_ref[g - SHARED:g - SHARED + 1, :] = whole_rows(rows[g], local_bits)
+    copy = pltpu.make_async_copy(place_ref, index_ref, sem)
+    copy.start()
+
+    @pl.when(position >= 0)
+    def _():
+        for g in range(SHARED):
+            start = (g ^ (FIRST_CHIP // 4)) * columns
+            out_ref[start:start + columns, :] = own_ref[start:start + columns, :]
+        matmul_all(rows, OWN_LOOKUPS, position, local_bits, columns, pair_ref, out_ref)
+
+    copy.wait()
+
+    @pl.when((position & 1) == 1)
+    def _():
+        for g in range(SHARED, OWN_LOOKUPS):
+            start = (g ^ (FIRST_CHIP // 4)) * columns
+            out_ref[start:start + columns, :] = own_ref[start:start + columns, :]
+
+    @pl.when((position & 1) == 0)
+    def _():
+        for g in range(SHARED, OWN_LOOKUPS):
+            lookup_group(rows[g], g, g - SHARED, position, local_bits, columns, index_ref, whole_ref, out_ref)
 
 
 def sum_kernel(scale, parts_ref, out_ref):
@@ -236,14 +263,18 @@
     half_shape = jax.ShapeDtypeStruct((samples * columns // LANES // 2, LANES), jnp.float32)
     work = samples * columns * length
     lookups = PARTNER_LOOKUPS + OWN_LOOKUPS
-    partner, own, pair = pl.pallas_call(
+    partner, own, pair, whole = pl.pallas_call(
         functools.partial(partner_kernel, local_bits),
-        out_shape=(half_shape, half_shape, jax.ShapeDtypeStruct((tiles * columns, 2 * LANES), jnp.bfloat16)),
+        out_shape=(
+            half_shape,
+            half_shape,
+            jax.ShapeDtypeStruct((tiles * columns, 2 * LANES), jnp.bfloat16),
+            jax.ShapeDtypeStruct((tiles * columns + 16, LANES), jnp.float32),
+        ),
         in_specs=[smem, vmem, vmem, vmem],
-        out_specs=(vmem, vmem, vmem),
+        out_specs=(vmem, vmem, vmem, vmem),
         scratch_shapes=[
             pltpu.VMEM((tiles, columns, LANES), jnp.float32),
-            pltpu.VMEM((tiles * columns + 16, LANES), jnp.float32),
             pltpu.VMEM((lookups, LANES), jnp.int32),
             pltpu.SMEM((lookups, LANES), jnp.int32),
             pltpu.SemaphoreType.DMA,
@@ -255,11 +286,16 @@
     own = pl.pallas_call(
         functools.partial(own_kernel, local_bits, columns),
         out_shape=half_shape,
-        in_specs=[smem, vmem, vmem, vmem],
+        in_specs=[smem, vmem, vmem, vmem, vmem],
         out_specs=vmem,
+        scratch_shapes=[
+            pltpu.VMEM((OWN_LOOKUPS - SHARED, LANES), jnp.int32),
+            pltpu.SMEM((OWN_LOOKUPS - SHARED, LANES), jnp.int32),
+            pltpu.SemaphoreType.DMA,
+        ],
         compiler_params=params,
         cost_estimate=pl.CostEstimate(flops=2 * work, bytes_accessed=2**21, transcendentals=0),
-    )(position, pair, own, sample_rows)
+    )(position, pair, whole, own, sample_rows)
     partial = own.reshape(chips, 4, LANES) + arrived
     order = [4 * (p ^ (FIRST_CHIP // 4)) + chip for p in range(chips // 4) for chip in CHIP_ORDER]
     parts = lax.all_to_all(partial, "rows", 0, 0, axis_index_groups=[[2 * chip + core for chip in order] for core in range(2)], tiled=True)

time: 23.3 us -> 23.2 us (level); the launches traced: 23.1 us -> 22.8 us
  starting transfers between devices: 1.5 us -> 1.09 us
    ppermute x1, starting transfers between devices: 1.5 us -> 1.09 us  [body(): lax.ppermute(partner.reshape(chips, 4, LANES), 'rows', [(i, i ^ 1) for i...]
  transfers between devices with their start and end apart: 1 -> 1, of which waited for: 0 -> 0; matrix products, arithmetic and copies ran while one was open for 0% -> 0% of each run, Pallas kernels for 5% -> 6%
where the time goes in v7:
time: 23.2 us; the launch traced here: 22.8 us
  blocking collectives  15.2 us (66%)
  Pallas kernels  5.07 us (22%)
  other arithmetic  1.36 us (6%)
  starting transfers between devices  1.09 us (5%)
    all_to_all x1, blocking collectives, body(): lax.all_to_all(partial, 'rows', 0, 0, axis_index_groups=[[2 * chip + core...  15.2 us
    pallas_call x1, Pallas kernels, body(): pl.pallas_call(functools.partial(partner_kernel, local_bits), out_shape=(...  3.08 us
    neg x1, other arithmetic, body(): -matrix_panel  1.33 us
    pallas_call x1, Pallas kernels, body(): pl.pallas_call(functools.partial(own_kernel, local_bits, columns), out_sh...  1.28 us
    ppermute x1, starting transfers between devices, body(): lax.ppermute(partner.reshape(chips, 4, LANES), 'rows', [(i, i ^ 1) for i...  1.09 us
    pallas_call x1, Pallas kernels, body(): pl.pallas_call(functools.partial(sum_kernel, -1.0 / math.sqrt(length * de...  0.7 us
  transfers between devices with their start and end apart: 1, of which 0 were waited for; matrix products, arithmetic and copies ran while one was open for 0% of the time, Pallas kernels for 6%

profile of v7, /device:TPU:1, one launch (start us, length us, event | category | flops | bytes accessed | tf_op | source)
XLA Modules:
  0.0 22.8 jit_solution(11390725627890471201)
XLA Ops:
  0.0 0.0 copy-start.1
  0.0 0.0 copy-start
  0.0 1.3 %neg.3.panel_ref = f32[16,16384]{1,0:T(8,128)S(1)} negate(f32[16,16384]{1,0:T(8,128)} %param.3) | non-fusion elementwise | flops 262144 | bytes 2097152 | tf_op jit(solution)/shard_map/neg | solution.py:284
  1.3 0.0 copy-done.1
  1.3 0.0 copy-done
  1.4 3.1 %shard_map.37 = (f32[256,128]{1,0:T(8,128)S(1)}, f32[256,128]{1,0:T(8,128)S(1)}, bf16[2048,256]{1,0:T(8,128)(2,1)S(1)}, f32[2064,128]{1,0:T(8,128)S(1)}) custom-call(s32[1]{0:T(128)} %bitcast.position_ref, f32[16,16384]{1,0:T(8,128)S(1)} %neg.3.panel_ref, s32[128,128]{1,0:T(8,128)S(1)} %bitcast.9, s32[32,128]{1,0:T(8,128)S(1)} %bitcast.10), custom_call_target="tpu_custom_call" | custom-call | flops 2147483648 | bytes 2097152 | tf_op jit(solution)/shard_map/pallas_call | solution.py:266
  4.4 1.1 %collective-permute-start = (f32[64,4,128]{2,1,0:T(4,128)S(1)}, f32[64,4,128]{2,1,0:T(4,128)S(1)}, u32[]{:S(2)}, u32[]{:S(2)}) collective-permute-start(f32[64,4,128]{2,1,0:T(4,128)S(1)} %bitcast.8), channel_id=1, source_target_pairs={{0,1},{1,0},{2,3},{3,2},{4,5},{5,4},{6,7},{7,6},{8,9},{9,8},{10,11... | collective-permute-start | bytes 393224 | tf_op jit(solution)/shard_map/ppermute | solution.py:285
  5.5 1.3 %shard_map.38 = f32[256,128]{1,0:T(8,128)S(1)} custom-call(s32[1]{0:T(128)} %bitcast.position_ref, bf16[2048,256]{1,0:T(8,128)(2,1)S(1)} %get-tuple-element.9.pair_ref, f32[2064,128]{1,0:T(8,128)S(1)} %get-tuple-element.10.whole_ref, f32[256,128]{1,0:T(8,128)S(1)} %get-tuple-element.11.own_ref, s32[32,128]{1,0:T(8,128)S(1)} %bitcast.11), custom_call_target="tpu_custom_call" | custom-call | flops 2147483648 | bytes 2097152 | tf_op jit(solution)/shard_map/pallas_call | solution.py:286
  6.8 0.0 collective-permute-done
  6.9 15.2 %all_to_all.5 = f32[64,4,128]{2,1,0:T(4,128)S(1)} all-to-all(f32[64,4,128]{2,1,0:T(4,128)S(1)} %add.3), channel_id=1, replica_groups={{116,112,118,114,124,120,126,122,100,96,102,98,108,104,110,106,84,80,86..., dimensions={0} | all-to-all | bytes 262144 | tf_op jit(solution)/shard_map/all_to_all | solution.py:301
  22.1 0.7 %shard_map.39 = f32[16,32]{1,0:T(8,128)} custom-call(f32[256,128]{1,0:T(8,128)S(1)} %bitcast.6), custom_call_target="tpu_custom_call" | custom-call | tf_op jit(solution)/shard_map/pallas_call | solution.py:302
  (1 shorter events, 0.0 us)
Async XLA Ops:
  0.0 1.3 %copy-start.1 = (s32[4096]{0:T(1024)S(1)}, s32[4096]{0:T(1024)}, u32[]{:S(2)}) copy-start(s32[4096]{0:T(1024)} %param.5) | copy-start | bytes 49156
  0.0 1.3 %copy-start = (s32[16384]{0:T(1024)S(1)}, s32[16384]{0:T(1024)}, u32[]{:S(2)}) copy-start(s32[16384]{0:T(1024)} %param.4) | copy-start | bytes 196612
  4.4 2.4 %collective-permute-start = (f32[64,4,128]{2,1,0:T(4,128)S(1)}, f32[64,4,128]{2,1,0:T(4,128)S(1)}, u32[]{:S(2)}, u32[]{:S(2)}) collective-permute-start(f32[64,4,128]{2,1,0:T(4,128)S(1)} %bitcast.8), channel_id=1, source_target_pairs={{0,1},{1,0},{2,3},{3,2},{4,5},{5,4},{6,7},{7,6},{8,9},{9,8},{10,11... | collective-permute-start | bytes 393224 | tf_op jit(solution)/shard_map/ppermute | solution.py:285

commit v8 on v7

--- a/solution.py
+++ b/solution.py
@@ -14,7 +14,7 @@
 FIRST_CHIP = 58
 UNROLL = 4
 PARTNER_LOOKUPS = 16
-OWN_LOOKUPS = 10
+OWN_LOOKUPS = 12
 SHARED = 6
 
 

time: 23.2 us -> 23.2 us (level)
  the two profiles are of different devices: /device:TPU:1 before, /device:TPU:0 now
where the time goes in v8:
time: 23.2 us; the launch traced here: 23.1 us
  blocking collectives  16.6 us (72%)
  Pallas kernels  4.95 us (21%)
  other arithmetic  1.36 us (6%)
    all_to_all x1, blocking collectives, body(): lax.all_to_all(partial, 'rows', 0, 0, axis_index_groups=[[2 * chip + core...  16.6 us
    pallas_call x1, Pallas kernels, body(): pl.pallas_call(functools.partial(partner_kernel, local_bits), out_shape=(...  2.68 us
    pallas_call x1, Pallas kernels, body(): pl.pallas_call(functools.partial(own_kernel, local_bits, columns), out_sh...  1.57 us
    neg x1, other arithmetic, body(): -matrix_panel  1.33 us
    pallas_call x1, Pallas kernels, body(): pl.pallas_call(functools.partial(sum_kernel, -1.0 / math.sqrt(length * de...  0.7 us
  transfers between devices with their start and end apart: 1, of which 0 were waited for; matrix products, arithmetic and copies ran while one was open for 0% of the time, Pallas kernels for 7%

profile of v8, /device:TPU:0, one launch (start us, length us, event | category | flops | bytes accessed | tf_op | source)
XLA Modules:
  0.0 23.1 jit_solution(1055238224047948212)
XLA Ops:
  0.0 0.0 copy-start.1
  0.0 0.0 copy-start
  0.0 1.3 %neg.3.panel_ref = f32[16,16384]{1,0:T(8,128)S(1)} negate(f32[16,16384]{1,0:T(8,128)} %param.3) | non-fusion elementwise | flops 262144 | bytes 2097152 | tf_op jit(solution)/shard_map/neg | solution.py:284
  1.3 0.0 copy-done.1
  1.3 0.0 copy-done
  1.4 2.7 %shard_map.37 = (f32[256,128]{1,0:T(8,128)S(1)}, f32[256,128]{1,0:T(8,128)S(1)}, bf16[2048,256]{1,0:T(8,128)(2,1)S(1)}, f32[2064,128]{1,0:T(8,128)S(1)}) custom-call(s32[1]{0:T(128)} %bitcast.position_ref, f32[16,16384]{1,0:T(8,128)S(1)} %neg.3.panel_ref, s32[128,128]{1,0:T(8,128)S(1)} %bitcast.9, s32[32,128]{1,0:T(8,128)S(1)} %bitcast.10), custom_call_target="tpu_custom_call" | custom-call | flops 2147483648 | bytes 2097152 | tf_op jit(solution)/shard_map/pallas_call | solution.py:266
  4.0 0.1 collective-permute-start
  4.1 1.6 %shard_map.38 = f32[256,128]{1,0:T(8,128)S(1)} custom-call(s32[1]{0:T(128)} %bitcast.position_ref, bf16[2048,256]{1,0:T(8,128)(2,1)S(1)} %get-tuple-element.9.pair_ref, f32[2064,128]{1,0:T(8,128)S(1)} %get-tuple-element.10.whole_ref, f32[256,128]{1,0:T(8,128)S(1)} %get-tuple-element.11.own_ref, s32[32,128]{1,0:T(8,128)S(1)} %bitcast.11), custom_call_target="tpu_custom_call" | custom-call | flops 2147483648 | bytes 2097152 | tf_op jit(solution)/shard_map/pallas_call | solution.py:286
  5.7 0.0 collective-permute-done
  5.8 16.6 %all_to_all.5 = f32[64,4,128]{2,1,0:T(4,128)S(1)} all-to-all(f32[64,4,128]{2,1,0:T(4,128)S(1)} %add.3), channel_id=1, replica_groups={{116,112,118,114,124,120,126,122,100,96,102,98,108,104,110,106,84,80,86..., dimensions={0} | all-to-all | bytes 262144 | tf_op jit(solution)/shard_map/all_to_all | solution.py:301
  22.4 0.7 %shard_map.39 = f32[16,32]{1,0:T(8,128)} custom-call(f32[256,128]{1,0:T(8,128)S(1)} %bitcast.6), custom_call_target="tpu_custom_call" | custom-call | tf_op jit(solution)/shard_map/pallas_call | solution.py:302
  (1 shorter events, 0.0 us)
Async XLA Ops:
  0.0 1.3 %copy-start.1 = (s32[4096]{0:T(1024)S(1)}, s32[4096]{0:T(1024)}, u32[]{:S(2)}) copy-start(s32[4096]{0:T(1024)} %param.5) | copy-start | bytes 49156
  0.0 1.3 %copy-start = (s32[16384]{0:T(1024)S(1)}, s32[16384]{0:T(1024)}, u32[]{:S(2)}) copy-start(s32[16384]{0:T(1024)} %param.4) | copy-start | bytes 196612
  4.0 1.7 %collective-permute-start = (f32[64,4,128]{2,1,0:T(4,128)S(1)}, f32[64,4,128]{2,1,0:T(4,128)S(1)}, u32[]{:S(2)}, u32[]{:S(2)}) collective-permute-start(f32[64,4,128]{2,1,0:T(4,128)S(1)} %bitcast.8), channel_id=1, source_target_pairs={{0,1},{1,0},{2,3},{3,2},{4,5},{5,4},{6,7},{7,6},{8,9},{9,8},{10,11... | collective-permute-start | bytes 393224 | tf_op jit(solution)/shard_map/ppermute | solution.py:285

commit v9 on v8

--- a/solution.py
+++ b/solution.py
@@ -15,7 +15,7 @@
 UNROLL = 4
 PARTNER_LOOKUPS = 16
 OWN_LOOKUPS = 12
-SHARED = 6
+SHARED = 5
 
 
 def butterflies(parts):

time: 23.2 us -> 23.2 us (level)
  no operation moved by 1% of the time
where the time goes in v9:
time: 23.2 us; the launch traced here: 23.1 us
  blocking collectives  16.6 us (72%)
  Pallas kernels  4.93 us (21%)
  other arithmetic  1.36 us (6%)
    all_to_all x1, blocking collectives, body(): lax.all_to_all(partial, 'rows', 0, 0, axis_index_groups=[[2 * chip + core...  16.6 us
    pallas_call x1, Pallas kernels, body(): pl.pallas_call(functools.partial(partner_kernel, local_bits), out_shape=(...  2.59 us
    pallas_call x1, Pallas kernels, body(): pl.pallas_call(functools.partial(own_kernel, local_bits, columns), out_sh...  1.63 us
    neg x1, other arithmetic, body(): -matrix_panel  1.33 us
    pallas_call x1, Pallas kernels, body(): pl.pallas_call(functools.partial(sum_kernel, -1.0 / math.sqrt(length * de...  0.7 us
  transfers between devices with their start and end apart: 1, of which 0 were waited for; matrix products, arithmetic and copies ran while one was open for 0% of the time, Pallas kernels for 7%

profile of v9, /device:TPU:0, one launch (start us, length us, event | category | flops | bytes accessed | tf_op | source)
XLA Modules:
  0.0 23.1 jit_solution(106832912471872040)
XLA Ops:
  0.0 0.0 copy-start.1
  0.0 0.0 copy-start
  0.0 1.3 %neg.3.panel_ref = f32[16,16384]{1,0:T(8,128)S(1)} negate(f32[16,16384]{1,0:T(8,128)} %param.3) | non-fusion elementwise | flops 262144 | bytes 2097152 | tf_op jit(solution)/shard_map/neg | solution.py:284
  1.3 0.0 copy-done.1
  1.3 0.0 copy-done
  1.4 2.6 %shard_map.37 = (f32[256,128]{1,0:T(8,128)S(1)}, f32[256,128]{1,0:T(8,128)S(1)}, bf16[2048,256]{1,0:T(8,128)(2,1)S(1)}, f32[2064,128]{1,0:T(8,128)S(1)}) custom-call(s32[1]{0:T(128)} %bitcast.position_ref, f32[16,16384]{1,0:T(8,128)S(1)} %neg.3.panel_ref, s32[128,128]{1,0:T(8,128)S(1)} %bitcast.9, s32[32,128]{1,0:T(8,128)S(1)} %bitcast.10), custom_call_target="tpu_custom_call" | custom-call | flops 2147483648 | bytes 2097152 | tf_op jit(solution)/shard_map/pallas_call | solution.py:266
  4.0 0.1 collective-permute-start
  4.0 1.6 %shard_map.38 = f32[256,128]{1,0:T(8,128)S(1)} custom-call(s32[1]{0:T(128)} %bitcast.position_ref, bf16[2048,256]{1,0:T(8,128)(2,1)S(1)} %get-tuple-element.9.pair_ref, f32[2064,128]{1,0:T(8,128)S(1)} %get-tuple-element.10.whole_ref, f32[256,128]{1,0:T(8,128)S(1)} %get-tuple-element.11.own_ref, s32[32,128]{1,0:T(8,128)S(1)} %bitcast.11), custom_call_target="tpu_custom_call" | custom-call | flops 2147483648 | bytes 2097152 | tf_op jit(solution)/shard_map/pallas_call | solution.py:286
  5.7 0.0 collective-permute-done
  5.7 16.6 %all_to_all.5 = f32[64,4,128]{2,1,0:T(4,128)S(1)} all-to-all(f32[64,4,128]{2,1,0:T(4,128)S(1)} %add.3), channel_id=1, replica_groups={{116,112,118,114,124,120,126,122,100,96,102,98,108,104,110,106,84,80,86..., dimensions={0} | all-to-all | bytes 262144 | tf_op jit(solution)/shard_map/all_to_all | solution.py:301
  22.4 0.7 %shard_map.39 = f32[16,32]{1,0:T(8,128)} custom-call(f32[256,128]{1,0:T(8,128)S(1)} %bitcast.6), custom_call_target="tpu_custom_call" | custom-call | tf_op jit(solution)/shard_map/pallas_call | solution.py:302
  (1 shorter events, 0.0 us)
Async XLA Ops:
  0.0 1.3 %copy-start.1 = (s32[4096]{0:T(1024)S(1)}, s32[4096]{0:T(1024)}, u32[]{:S(2)}) copy-start(s32[4096]{0:T(1024)} %param.5) | copy-start | bytes 49156
  0.0 1.3 %copy-start = (s32[16384]{0:T(1024)S(1)}, s32[16384]{0:T(1024)}, u32[]{:S(2)}) copy-start(s32[16384]{0:T(1024)} %param.4) | copy-start | bytes 196612
  4.0 1.7 %collective-permute-start = (f32[64,4,128]{2,1,0:T(4,128)S(1)}, f32[64,4,128]{2,1,0:T(4,128)S(1)}, u32[]{:S(2)}, u32[]{:S(2)}) collective-permute-start(f32[64,4,128]{2,1,0:T(4,128)S(1)} %bitcast.8), channel_id=1, source_target_pairs={{0,1},{1,0},{2,3},{3,2},{4,5},{5,4},{6,7},{7,6},{8,9},{9,8},{10,11... | collective-permute-start | bytes 393224 | tf_op jit(solution)/shard_map/ppermute | solution.py:285
